TPU v7x, 128 devices: a whole 4x4x4 slice. The times are simulated.
128 devices in a mesh: cp: 8 (over x, core), dp: 16 (over y, z).
Axes of the slice: x: 4, y: 4, z: 4, core: 2. Of those that a mesh axis runs over, the one named last changes fastest.
Arguments:
- q_nope: bfloat16 [2, 16, 1024, 32, 128], P(None, 'dp', 'cp'), may hold values from -3 to 3
- q_rope: bfloat16 [2, 16, 1024, 2048], P(None, 'dp', 'cp'), may hold values from -310 to 310, as said below
- grad_out: bfloat16 [2, 16, 1024, 32, 128], P(None, 'dp', 'cp'), may hold values from -6 to 6
- latent: bfloat16 [16, 1024, 512], P('dp', 'cp'), may hold values from -6 to 6
- key_rope: bfloat16 [16, 64, 1024], P('dp', None, 'cp'), may hold values from -6 to 6
- hidden_in: bfloat16 [16, 1024, 7168], P('dp', 'cp'), may hold values from -6 to 6
- w_uk: bfloat16 [2, 32, 128, 512], replicated, may hold values from -0.5 to 0.5
- w_uv: bfloat16 [2, 32, 512, 128], replicated, may hold values from -0.25 to 0.25
- doc_lengths: int32 [16, 32], P('dp'), may hold values from 1 to 192, 1024 in all within a row
- plan: int32 [16, 8, 8], P('dp'), may hold values from 0 to 7, each once within a row
Outputs:
- dq_nope: bfloat16 [2, 16, 1024, 32, 128], P(None, 'dp', 'cp')
- dq_rope: bfloat16 [2, 16, 1024, 2048], P(None, 'dp', 'cp')
- d_latent: bfloat16 [16, 1024, 512], P('dp', 'cp')
- d_key_rope: bfloat16 [16, 64, 1024], P('dp', None, 'cp')
- d_wdkv: float32 [7168, 576], P(('cp', 'dp'))
Inputs may be any that keep to these rules, and one draw needn't show every extreme that they name: `q_rope`: in the hidden draw some queries point strongly at nearby keys. `doc_lengths`: each packed batch holds 32 documents that fill its 1024 tokens; the longest has exactly 192 tokens. Each row plan[p, d] is a permutation of 0 to 7.
All inputs are finite; a program needn't handle non-finite values.
Results may differ from a plain program's by a relative error of at most 0.009.
Values may be sent and summed in bfloat16 or wider, within the bound.
A program may use at most 192 MiB of HBM per device.

v0:
```python
import math

import jax
import jax.numpy as jnp
from jax import lax
from jax.sharding import PartitionSpec as P

MAXDOC = 192


def doc_numbers(lengths, count):
    ends = jnp.cumsum(lengths)
    places = jnp.arange(count, dtype=jnp.int32)
    return jnp.sum((places[:, None] >= ends[None, :]).astype(jnp.int32), axis=1)


def arrange(values, order, pieces):
    blocks = values.reshape((values.shape[0], pieces, values.shape[1] // pieces) + values.shape[2:])
    return jnp.take(blocks, order, axis=1).reshape(values.shape)


def attend(q_part, r_part, g_part, starts, length, lat_pad, rope_pad, ids_pad, w_uk, w_uv, margin):
    nblk = starts.shape[0]
    span = margin + length
    layers = q_part.shape[0]
    heads = q_part.shape[2]
    rope = rope_pad.shape[0]
    bf16 = jnp.bfloat16
    f32 = jnp.float32
    scale = 1.0 / math.sqrt(q_part.shape[3] + rope)

    def cut(start):
        return (
            lax.dynamic_slice_in_dim(lat_pad, start, span, 0),
            lax.dynamic_slice_in_dim(rope_pad, start, span, 1),
            lax.dynamic_slice_in_dim(ids_pad, start, span, 0),
        )

    lat_win, rope_win, ids_win = jax.vmap(cut)(starts)
    allowed = (ids_win[:, None, :] == ids_win[:, margin:, None]) & (
        jnp.arange(span)[None, None, :] <= margin + jnp.arange(length)[None, :, None]
    )
    lat_acc = jnp.zeros((nblk, span, lat_pad.shape[1]), f32)
    rope_acc = jnp.zeros((nblk, span, rope), f32)
    nope_list = []
    rot_list = []
    for layer in range(layers):
        q_lat = jnp.einsum(
            "rhd,hdl->rhl", q_part[layer], w_uk[layer], preferred_element_type=f32
        ).astype(bf16)
        q_lat = q_lat.reshape(nblk, length, heads, -1)
        q_rot = r_part[layer].reshape(nblk, length, heads, rope)
        score = jnp.einsum("bqhl,bkl->bhqk", q_lat, lat_win, preferred_element_type=f32)
        score = (
            score + jnp.einsum("bqhr,brk->bhqk", q_rot, rope_win, preferred_element_type=f32)
        ) * scale
        score = jnp.where(allowed[:, None], score, -jnp.inf)
        top = jnp.max(score, axis=3, keepdims=True)
        expd = jnp.exp(score - top)
        prob = expd / jnp.sum(expd, axis=3, keepdims=True)
        g_lat = jnp.einsum(
            "rhd,hld->rhl", g_part[layer], w_uv[layer], preferred_element_type=f32
        ).astype(bf16)
        g_lat = g_lat.reshape(nblk, length, heads, -1)
        dprob = jnp.einsum("bqhl,bkl->bhqk", g_lat, lat_win, preferred_element_type=f32)
        delta = jnp.sum(prob * dprob, axis=3, keepdims=True)
        dscore = (prob * (dprob - delta) * scale).astype(bf16)
        prob_low = prob.astype(bf16)
        dq_lat = jnp.einsum("bhqk,bkl->bqhl", dscore, lat_win, preferred_element_type=f32).astype(
            bf16
        )
        dq_lat = dq_lat.reshape(nblk * length, heads, -1)
        nope_list.append(
            jnp.einsum("rhl,hdl->rhd", dq_lat, w_uk[layer], preferred_element_type=f32).astype(bf16)
        )
        rotary = jnp.einsum("bhqk,brk->bqhr", dscore, rope_win, preferred_element_type=f32).astype(
            bf16
        )
        rot_list.append(rotary.reshape(nblk * length, heads * rope))
        lat_acc = lat_acc + jnp.einsum("bhqk,bqhl->bkl", dscore, q_lat, preferred_element_type=f32)
        lat_acc = lat_acc + jnp.einsum(
            "bhqk,bqhl->bkl", prob_low, g_lat, preferred_element_type=f32
        )
        rope_acc = rope_acc + jnp.einsum(
            "bhqk,bqhr->bkr", dscore, q_rot, preferred_element_type=f32
        )

    def add_window(index, totals):
        lat_total, rope_total = totals
        start = starts[index]
        piece = lax.dynamic_slice_in_dim(lat_total, start, span, 0) + lat_acc[index]
        lat_total = lax.dynamic_update_slice_in_dim(lat_total, piece, start, 0)
        piece = lax.dynamic_slice_in_dim(rope_total, start, span, 0) + rope_acc[index]
        rope_total = lax.dynamic_update_slice_in_dim(rope_total, piece, start, 0)
        return (lat_total, rope_total)

    whole = lat_pad.shape[0]
    lat_total, rope_total = lax.fori_loop(
        0,
        nblk,
        add_window,
        (jnp.zeros((whole, lat_pad.shape[1]), f32), jnp.zeros((whole, rope), f32)),
    )
    return (jnp.stack(nope_list), jnp.stack(rot_list), lat_total[margin:], rope_total[margin:])


def on_device(q_nope, q_rope, grad_out, latent, key_rope, hidden_in, w_uk, w_uv, doc_lengths, plan):
    groups = lax.axis_size("cp")
    mine = lax.axis_index("cp")
    local = latent.shape[1]
    length = local // groups
    total = local * groups
    margin = MAXDOC
    lat_all, rope_all = (
        lax.all_gather(latent[0], "cp", axis=0, tiled=True),
        lax.all_gather(key_rope[0], "cp", axis=1, tiled=True),
    )
    lat_pad = jnp.concatenate(
        [jnp.zeros((margin, lat_all.shape[1]), lat_all.dtype), lat_all], axis=0
    )
    rope_pad = jnp.concatenate(
        [jnp.zeros((rope_all.shape[0], margin), rope_all.dtype), rope_all], axis=1
    )
    ids_pad = jnp.concatenate(
        [jnp.full((margin,), -1, jnp.int32), doc_numbers(doc_lengths[0], total)]
    )
    table = plan[0]
    order = table[mine]
    q_part, r_part, g_part = (
        lax.all_to_all(
            arrange(q_nope[:, 0], order, groups), "cp", split_axis=1, concat_axis=1, tiled=True
        ),
        lax.all_to_all(
            arrange(q_rope[:, 0], order, groups), "cp", split_axis=1, concat_axis=1, tiled=True
        ),
        lax.all_to_all(
            arrange(grad_out[:, 0], order, groups), "cp", split_axis=1, concat_axis=1, tiled=True
        ),
    )
    starts = jnp.arange(groups, dtype=jnp.int32) * local + table[:, mine] * length
    gq_nope, gq_rope, lat_total, rope_total = attend(
        q_part, r_part, g_part, starts, length, lat_pad, rope_pad, ids_pad, w_uk, w_uv, margin
    )
    lat_sum, rope_sum = (
        lax.psum_scatter(lat_total, "cp", scatter_dimension=0, tiled=True),
        lax.psum_scatter(rope_total, "cp", scatter_dimension=0, tiled=True),
    )
    d_latent = lat_sum.astype(jnp.bfloat16)
    rope_low = rope_sum.astype(jnp.bfloat16)
    joined = jnp.concatenate([d_latent, rope_low], axis=1)
    inputs = hidden_in[0]
    d_wdkv = lax.psum_scatter(
        lax.dot_general(
            inputs, joined, (((0,), (0,)), ((), ())), preferred_element_type=jnp.float32
        ),
        ("cp", "dp"),
        scatter_dimension=0,
        tiled=True,
    )
    return (
        gq_nope[:, None],
        gq_rope[:, None],
        d_latent[None],
        jnp.transpose(rope_low)[None],
        d_wdkv,
    )


def solution(mesh):
    placed = (
        P(None, "dp", "cp", None, None),
        P(None, "dp", "cp", None),
        P(None, "dp", "cp", None, None),
        P("dp", "cp", None),
        P("dp", None, "cp"),
        P("dp", "cp", None),
        P(),
        P(),
        P("dp", None),
        P("dp", None, None),
    )
    return jax.shard_map(
        on_device,
        mesh=mesh,
        in_specs=placed,
        out_specs=(
            P(None, "dp", "cp", None, None),
            P(None, "dp", "cp", None),
            P("dp", "cp", None),
            P("dp", None, "cp"),
            P(("cp", "dp"), None),
        ),
        check_vma=False,
    )
```

profile of v0, /device:TPU:1, one launch (start us, length us, event | category | flops | bytes accessed | tf_op | source)
XLA Modules:
  0.0 687.4 jit_solution(16912496341261480895)
XLA Ops:
  9.5 1.8 gather_fusion
  11.6 2.0 copy.127
  13.7 5.8 all-to-all-start.1
  20.1 2.2 gather_fusion.2
  22.3 4.0 gather_fusion.1
  26.2 4.1 select_bitcast_fusion.1
  30.3 15.1 %all-gather.1 = bf16[1,64,1024]{2,1,0:T(8,128)(2,1)S(1)} all-gather(bf16[1,64,128]{2,1,0:T(8,128)(2,1)S(1)} %copy-done.16), channel_id=3, replica_groups=mesh['cp'=8,'dp'=16] {'cp'}, dimensions={2}, use_global_device_ids=true | all-gather | bytes 147456 | tf_op jit(solution)/shard_map/all_gather | solution.py:116
  45.5 9.7 %while.20 = (s32[]{:T(128)}, s32[1216]{0:T(1024)S(1)}, s32[8,1]{0,1:T(1,128)S(1)}, s32[8,208]{1,0:T(8,128)S(1)}, s32[]{:T(128)}, /*index=5*/s32[]{:T(128)}) while((s32[]{:T(128)}, s32[1216]{0:T(1024)S(1)}, s32[8,1]{0,1:T(1,128)S(1)}, s32[8,208]{1,0:T(8,128)S(1)}, s32[]{:T(128)}, /*index=5*/s32[]{:T(128)}) %tuple.89), condition=%wide.while_cond.1, body=%wide.while_body.1.sunk | while | flops 2 | bytes 3425 | solution.py:36
  55.3 2.2 copy.122
  57.5 2.1 copy.123
  60.1 2.1 copy.129
  62.4 4.4 all-to-all-start.2
  66.8 10.6 %while.21 = (s32[]{:T(128)}, bf16[64,1216]{1,0:T(8,128)(2,1)S(1)}, s32[8,2]{0,1:T(2,128)S(1)}, bf16[8,64,208]{2,1,0:T(8,128)(2,1)S(1)}, s32[]{:T(128)}) while((s32[]{:T(128)}, bf16[64,1216]{1,0:T(8,128)(2,1)S(1)}, s32[8,2]{0,1:T(2,128)S(1)}, bf16[8,64,208]{2,1,0:T(8,128)(2,1)S(1)}, s32[]{:T(128)}) %tuple.92), condition=%wide.while_cond.2, body=%wide.while_body.2.sunk | while | flops 2 | bytes 65641 | solution.py:35
  77.4 6.3 slice_reduce_fusion.1
  83.7 2.8 reshape_squeeze.17
  86.5 2.8 reshape_squeeze.19
  89.3 1.3 concatenate.18
  90.6 2.7 all-to-all-done.2
  93.3 5.1 all-to-all-start
  98.4 2.9 fusion.128
  101.3 5.5 fusion.55
  106.8 11.0 %while.19 = (s32[]{:T(128)}, bf16[1216,512]{1,0:T(8,128)(2,1)S(1)}, s32[8,2]{0,1:T(2,128)S(1)}, bf16[8,208,512]{2,1,0:T(8,128)(2,1)S(1)}, s32[]{:T(128)}) while((s32[]{:T(128)}, bf16[1216,512]{1,0:T(8,128)(2,1)S(1)}, s32[8,2]{0,1:T(2,128)S(1)}, bf16[8,208,512]{2,1,0:T(8,128)(2,1)S(1)}, s32[]{:T(128)}) %tuple.86), condition=%wide.while_cond, body=%wide.while_body.sunk | while | flops 2 | bytes 426089 | solution.py:34
  117.7 7.1 %fusion.28 = f32[8,208,16,32]{1,3,2,0:T(8,128)} fusion(bf16[8,16,32,512]{3,1,0,2:T(8,128)(2,1)} %bitcast.299, bf16[8,208,512]{2,1,0:T(8,128)(2,1)S(1)} %get-tuple-element.125), kind=kOutput, calls=%fused_computation.49 | convolution fusion | flops 872415232 | bytes 9306112 | tf_op jit(solution)/shard_map/bqhl,bkl->bhqk/dot_general | solution.py:65
  124.9 2.9 fusion.127
  127.8 3.4 fusion.52
  131.2 3.0 fusion.32
  135.0 3.1 fusion.130
  138.3 16.8 %fusion.26 = f32[8,208,512,1]{2,1,3,0:T(8,128)} fusion(bf16[8,16,32,512]{3,1,0,2:T(8,128)(2,1)} %bitcast.300, f32[8,32,16]{1,2,0:T(8,128)S(1)} %get-tuple-element.256, f32[8,32,16,208]{3,1,2,0:T(8,128)} %copy-done.3), kind=kOutput, calls=%fused_computation.47 | convolution fusion | flops 874975424 | bytes 11026432 | tf_op jit(solution)/shard_map/bhqk,bqhl->bkl/dot_general | solution.py:81
  155.1 33.3 %fusion.30 = f32[8,208,512,1]{2,1,3,0:T(8,128)} fusion(bf16[8,16,32,512]{3,1,0,2:T(8,128)(2,1)} %bitcast.304, f32[8,208,16,32]{1,3,2,0:T(8,128)} %fusion.28, f32[8,32,16,208]{3,1,2,0:T(8,128)} %get-tuple-element.257, f32[8,32,16]{1,2,0:T(8,128)S(1)} %get-tuple-element.256), kind=kOutput, calls=%fused_computation.51 | convolution fusion | flops 878383296 | bytes 14434304 | tf_op jit(solution)/shard_map/bhqk,bqhl->bkl/dot_general | solution.py:80
  188.4 30.3 %fusion.99 = f32[8,208,64]{1,2,0:T(8,128)} fusion(bf16[8,16,32,64]{3,2,1,0:T(8,128)(2,1)S(1)} %copy-done.10, f32[8,208,16,32]{1,3,2,0:T(8,128)} %fusion.28, f32[8,32,16,208]{3,1,2,0:T(8,128)} %get-tuple-element.257, f32[8,32,16]{1,2,0:T(8,128)S(1)} %get-tuple-element.256), kind=kOutput, calls=%fused_computation.104 | convolution fusion | flops 115019984 | bytes 7782400 | tf_op jit(solution)/shard_map/bhqk,bqhr->bkr/dot_general | solution.py:84
  218.8 3.8 fusion.49
  222.7 5.0 fusion.46
  227.7 4.9 fusion.36
  232.6 3.0 fusion.40
  236.4 3.0 fusion.131
  239.6 17.1 %fusion.34 = f32[8,208,512,1]{2,1,3,0:T(8,128)} fusion(bf16[8,16,32,512]{3,1,0,2:T(8,128)(2,1)} %bitcast.306, f32[8,32,16]{1,2,0:T(8,128)S(1)} %get-tuple-element.258, f32[8,32,16,208]{3,1,2,0:T(8,128)} %copy-done.2), kind=kOutput, calls=%fused_computation.55 | convolution fusion | flops 874975424 | bytes 11026432 | tf_op jit(solution)/shard_map/bhqk,bqhl->bkl/dot_general | solution.py:81
  256.7 30.3 %fusion.101 = f32[8,208,64]{1,2,0:T(8,128)} fusion(f32[8,208,64]{1,2,0:T(8,128)} %fusion.99, bf16[8,16,32,64]{3,2,1,0:T(8,128)(2,1)S(1)} %copy-done.9, f32[8,208,16,32]{1,3,2,0:T(8,128)} %fusion.36, f32[8,32,16,208]{3,1,2,0:T(8,128)} %get-tuple-element.259, f32[8,32,16]{1,2,0:T(8,128)S(1)} %get-tuple-element.258), kind=kOutput, calls=%fused_computation.106 | convolution fusion | flops 115126480 | bytes 8208384 | tf_op jit(solution)/shard_map/bhqk,bqhr->bkr/dot_general | solution.py:84
  287.0 33.3 %bitcast_add_fusion.2 = f32[8,208,512]{2,1,0:T(8,128)} fusion(f32[8,208,512,1]{2,1,3,0:T(8,128)} %fusion.26, f32[8,208,512,1]{2,1,3,0:T(8,128)} %fusion.30, f32[8,208,512,1]{2,1,3,0:T(8,128)} %fusion.34, bf16[8,16,32,512]{3,1,0,2:T(8,128)(2,1)} %bitcast.302, f32[8,208,16,32]{1,3,2,0:T(8,128)} %fusion.36, f32[8,32,16,208]{3,1,2,0:T(8,128)} %get-tuple-element.259, ...), kind=kOutput, calls=%fused_computation.67 | convolution fusion | flops 880939200 | bytes 24657920 | tf_op jit(solution)/shard_map/bhqk,bqhl->bkl/dot_general | solution.py:80
  320.4 1.8 broadcast_in_dim.85
  322.1 61.1 %while.18 = (s32[]{:T(128)}, f32[1216,512]{1,0:T(8,128)}, f32[1216,64]{0,1:T(8,128)S(1)}, s32[8]{0:T(128)S(1)}, f32[8,208,512]{2,1,0:T(8,128)}, /*index=5*/f32[8,208,64]{1,2,0:T(8,128)}, s32[]{:T(128)}, s32[]{:T(128)}, s32[]{:T(128)}) while((s32[]{:T(128)}, f32[1216,512]{1,0:T(8,128)}, f32[1216,64]{0,1:T(8,128)S(1)}, s32[8]{0:T(128)S(1)}, ...), condition=%wide.region_9.11_spmd, body=%wide.region_8.10_spmd.sunk | while | flops 119813 | bytes 2928811 | solution.py:98
  326.8 1.2 bitcast_add_fusion.8
  328.0 1.8 dynamic_update_slice.16
  334.3 1.2 bitcast_add_fusion.8
  335.5 1.8 dynamic_update_slice.16
  343.2 1.8 dynamic_update_slice.16
  350.9 1.8 dynamic_update_slice.16
  358.5 1.9 dynamic_update_slice.16
  366.2 1.9 dynamic_update_slice.16
  373.9 1.8 dynamic_update_slice.16
  381.4 1.9 dynamic_update_slice.16
  384.1 3.1 slice.52
  387.5 26.8 %reduce-scatter.6.cloned.1.call-done = f32[128,64]{0,1:T(8,128)} async-done(((f32[1024,64]{0,1:T(8,128)}), f32[128,64]{0,1:T(8,128)}) %reduce-scatter.6.cloned.1.call-update) | async-done | bytes 32784 | tf_op jit(solution)/shard_map/reduce_scatter | solution.py:146
  415.1 34.4 %reduce-scatter.4.cloned.1.call-done = f32[128,512]{1,0:T(8,128)} async-done(((f32[1024,512]{1,0:T(8,128)}), f32[128,512]{1,0:T(8,128)}) %reduce-scatter.4.cloned.1.call-update) | async-done | bytes 262160 | tf_op jit(solution)/shard_map/reduce_scatter | solution.py:145
  450.5 9.5 %convolution_bitcast_fusion = f32[7168,576]{0,1:T(8,128)} fusion(bf16[1,128,7168]{2,1,0:T(8,128)(2,1)} %param.19, bf16[128,64]{1,0:T(8,128)(2,1)S(1)} %copy.144, bf16[128,512]{1,0:T(8,128)(2,1)S(1)} %convert_element_type.106), kind=kOutput, calls=%fused_computation.16 | convolution fusion | flops 1057259520 | bytes 18497536 | tf_op jit(solution)/shard_map/dot_general | solution.py:153
  461.0 29.2 %fusion.88 = bf16[8,16,32,64]{3,2,1,0:T(8,128)(2,1)} fusion(f32[8,208,16,32]{1,3,2,0:T(8,128)} %fusion.28, bf16[8,64,208]{2,1,0:T(8,128)(2,1)S(1)} %copy-done.13, f32[8,32,16,208]{3,1,2,0:T(8,128)} %get-tuple-element.257, f32[8,32,16]{1,2,0:T(8,128)S(1)} %get-tuple-element.256), kind=kOutput, calls=%fused_computation.101 | convolution fusion | flops 115282128 | bytes 7569408 | tf_op jit(solution)/shard_map/bhqk,brk->bqhr/dot_general | solution.py:76
  490.2 2.1 stack_reshape.7
  492.3 29.1 %fusion.87 = bf16[8,16,32,64]{3,2,1,0:T(8,128)(2,1)} fusion(f32[8,208,16,32]{1,3,2,0:T(8,128)} %fusion.36, bf16[8,64,208]{2,1,0:T(8,128)(2,1)S(1)} %copy-done.13, f32[8,32,16,208]{3,1,2,0:T(8,128)} %get-tuple-element.259, f32[8,32,16]{1,2,0:T(8,128)S(1)} %get-tuple-element.258), kind=kOutput, calls=%fused_computation.100 | convolution fusion | flops 115282128 | bytes 7569408 | tf_op jit(solution)/shard_map/bhqk,brk->bqhr/dot_general | solution.py:76
  521.4 2.1 stack_reshape.6
  523.5 29.5 %convolution_convert_fusion = bf16[8,512,32,16]{1,2,3,0:T(8,128)(2,1)} fusion(f32[8,208,16,32]{1,3,2,0:T(8,128)} %fusion.28, bf16[8,208,512]{2,1,0:T(8,128)(2,1)S(1)} %get-tuple-element.125, f32[8,32,16,208]{3,1,2,0:T(8,128)} %get-tuple-element.257, f32[8,32,16]{1,2,0:T(8,128)S(1)} %get-tuple-element.256), kind=kOutput, calls=%fused_computation.74 | convolution fusion | flops 880480448 | bytes 12730368 | tf_op jit(solution)/shard_map/bhqk,bkl->bqhl/dot_general | solution.py:69
  553.0 29.6 %convolution_convert_fusion.1 = bf16[8,512,32,16]{1,2,3,0:T(8,128)(2,1)} fusion(f32[8,208,16,32]{1,3,2,0:T(8,128)} %fusion.36, bf16[8,208,512]{2,1,0:T(8,128)(2,1)S(1)} %get-tuple-element.125, f32[8,32,16,208]{3,1,2,0:T(8,128)} %get-tuple-element.259, f32[8,32,16]{1,2,0:T(8,128)S(1)} %get-tuple-element.258), kind=kOutput, calls=%fused_computation.75 | convolution fusion | flops 880480448 | bytes 12730368 | tf_op jit(solution)/shard_map/bhqk,bkl->bqhl/dot_general | solution.py:69
  582.6 6.3 fusion.89
  588.9 5.1 fusion.94
  594.2 2.7 copy.145
  599.2 79.4 %all-reduce.8.cloned.1.call-done = f32[7168,576]{0,1:T(8,128)} async-done(((f32[7168,576]{0,1:T(8,128)}), f32[7168,576]{0,1:T(8,128)}) %all-reduce.8.cloned.1.call-update) | async-done | bytes 16515088
  (232 shorter events, 73.0 us)
Async XLA Ops:
  7.2 12.9 %copy-start = (bf16[2,1,128,32,128]{4,3,2,1,0:T(8,128)(2,1)S(1)}, bf16[2,1,128,32,128]{4,3,2,1,0:T(8,128)(2,1)}, u32[]{:S(2)}) copy-start(bf16[2,1,128,32,128]{4,3,2,1,0:T(8,128)(2,1)} %param.16) | copy-start | bytes 6291460
  7.2 82.1 %all-gather.4.cloned.1.call-start = ((), (), s32[]{:S(2)}) async-start(), calls=%async_computation.7 | async-start | bytes 1179648 | tf_op jit(solution)/shard_map/all_gather | solution.py:115
  11.3 8.2 %copy-start.17 = (s32[1,8,8]{2,1,0:T(8,128)S(1)}, s32[1,8,8]{2,1,0:T(8,128)}, u32[]{:S(2)}) copy-start(s32[1,8,8]{2,1,0:T(8,128)} %param.23) | copy-start | bytes 772
  11.3 8.4 %copy-start.18 = (s32[1,32]{1,0:T(1,128)S(1)}, s32[1,32]{1,0:T(1,128)}, u32[]{:S(2)}) copy-start(s32[1,32]{1,0:T(1,128)} %param.22) | copy-start | bytes 388
  13.7 48.7 %all-to-all-start.1 = ((bf16[2,128,2048]{2,0,1:T(2,128)(2,1)}), bf16[2,128,2048]{2,0,1:T(2,128)(2,1)S(1)}, u32[]{:S(2)}, u32[]{:S(2)}) async-start(bf16[2,128,2048]{2,0,1:T(2,128)(2,1)} %copy.127), calls=%async_computation.1 | async-start | bytes 2097152 | tf_op jit(solution)/shard_map/all_to_all | solution.py:133
  22.3 4.0 copy-start.8
  26.2 4.1 copy-start.16
  55.3 4.3 copy-start.7
  62.4 30.9 %all-to-all-start.2 = ((bf16[2,128,32,128]{3,2,0,1:T(8,128)(2,1)}), bf16[2,128,32,128]{3,2,0,1:T(8,128)(2,1)}, u32[]{:S(2)}, u32[]{:S(2)}) async-start(bf16[2,128,32,128]{3,2,0,1:T(8,128)(2,1)} %copy.129), calls=%async_computation.2 | async-start | bytes 4194304 | tf_op jit(solution)/shard_map/all_to_all | solution.py:136
  77.4 158.2 %copy-start.12 = (bf16[8,64,208]{2,1,0:T(8,128)(2,1)}, bf16[8,64,208]{2,1,0:T(8,128)(2,1)S(1)}, u32[]{:S(2)}) copy-start(bf16[8,64,208]{2,1,0:T(8,128)(2,1)S(1)} %get-tuple-element.141) | copy-start | bytes 638980
  93.3 31.6 %all-to-all-start = ((bf16[2,128,32,128]{3,2,0,1:T(8,128)(2,1)}), bf16[2,128,32,128]{3,2,0,1:T(8,128)(2,1)}, u32[]{:S(2)}, u32[]{:S(2)}) async-start(bf16[2,128,32,128]{3,2,0,1:T(8,128)(2,1)} %copy.123), calls=%async_computation | async-start | bytes 4194304 | tf_op jit(solution)/shard_map/all_to_all | solution.py:130
  98.4 315.8 %reduce-scatter.6.cloned.1.call-start = ((), (), s32[]{:S(2)}) async-start(), calls=%async_computation.6 | async-start | bytes 294912 | tf_op jit(solution)/shard_map/reduce_scatter | solution.py:146
  131.2 3.0 copy-start.5
  131.2 3.0 copy-start.10
  135.0 3.3 copy-start.3
  218.8 3.9 copy-start.11
  222.7 5.0 copy-start.6
  227.6 5.0 copy-start.4
  232.6 3.0 copy-start.9
  236.4 3.3 copy-start.2
  384.1 65.4 %reduce-scatter.4.cloned.1.call-start = ((), (), s32[]{:S(2)}) async-start(), calls=%async_computation.5 | async-start | bytes 2359296 | tf_op jit(solution)/shard_map/reduce_scatter | solution.py:145
  387.2 291.4 %all-reduce.8.cloned.1.call-start = ((), (), s32[]{:S(2)}) async-start(), calls=%async_computation.8 | async-start | bytes 33030144
  460.0 0.9 copy-start.13
  582.6 6.3 copy-start.19
  594.0 86.7 %copy-start.1 = (bf16[2,1,128,32,128]{4,3,2,1,0:T(8,128)(2,1)S(1)}, bf16[2,1,128,32,128]{4,3,2,1,0:T(8,128)(2,1)}, u32[]{:S(2)}) copy-start(bf16[2,1,128,32,128]{4,3,2,1,0:T(8,128)(2,1)} %param.16) | copy-start | bytes 6291460
  594.2 3.8 copy-start.15
  594.2 4.4 copy-start.14
Sparse Core Ops, SparseCore 0:
  9.7 31.4 all-gather.3
  384.2 29.9 reduce-scatter.5
  417.3 32.1 reduce-scatter.3
  460.2 218.4 all-reduce.7
where the time goes:
time: 699 us; the launch traced here: 687 us
  matrix products  337 us (48%)
  waiting for transfers between devices  144 us (21%)
  local copies, waits for them, and re-layouts  118 us (17%)
  other arithmetic  26.6 us (4%)
  loops' own time  16.6 us (2%)
  starting transfers between devices  15.6 us (2%)
  blocking collectives  15.1 us (2%)
  between operations  14.4 us (2%)
    unnamed x5, waiting for transfers between devices  80.2 us
    dot_general x2, matrix products, attend(): jnp.einsum('bhqk,bqhl->bkl', dscore, q_lat, preferred_element_type=f32)  66.7 us
    dot_general x2, matrix products, attend(): jnp.einsum('bhqk,bqhr->bkr', dscore, q_rot, preferred_element_type=f32)  60.6 us
    dot_general x2, matrix products, attend(): jnp.einsum('bhqk,bkl->bqhl', dscore, lat_win, preferred_element_type=f32)  59.1 us
    dot_general x2, matrix products, attend(): jnp.einsum('bhqk,brk->bqhr', dscore, rope_win, preferred_element_type=f32)  58.4 us
    reduce_scatter x1, waiting for transfers between devices, on_device(): lax.psum_scatter(lat_total, 'cp', scatter_dimension=0, tiled=True)  34.4 us
    dot_general x2, matrix products, attend(): jnp.einsum('bhqk,bqhl->bkl', prob_low, g_lat, preferred_element_type=f32)  33.9 us
    gather x72, local copies, waits for them, and re-layouts  30.4 us
  transfers between devices with their start and end apart: 7, of which 4 were waited for; matrix products, arithmetic and copies ran while one was open for 33% of the time, Pallas kernels for 0%

commit v1 on v0

v1 whole, which is shorter than its diff:
```python
import functools
import math

import jax
import jax.numpy as jnp
from jax import lax
from jax.experimental import pallas as pl
from jax.experimental.pallas import tpu as pltpu
from jax.sharding import PartitionSpec as P

BF = jnp.bfloat16
F32 = jnp.float32
MARGIN = 192
SUB = 64
WIN = 256
HG = 8


def dot(a, b, ca, cb):
    return lax.dot_general(a, b, (((ca,), (cb,)), ((), ())), preferred_element_type=F32)


def attention(
    lens, order, qn_h, qr_h, go_h, le_h, wk_h, wv_h,
    on, orp, acc,
    qn, qr, go, le, wk, wv, qf, gf, of, ro, ql, gl, dq, bias, sem_q, sem_w,
):
    layers, rows, head = qn.shape
    tok = qr.shape[1]
    heads = rows // tok
    lat = gl.shape[2]
    steps = heads // HG
    blk = tok // on.shape[0]
    scale = 1.0 / math.sqrt(head + 64)
    me = lax.axis_index("cp")

    def q_copies(layer):
        return [
            pltpu.make_async_copy(qn_h.at[layer], qn.at[layer], sem_q.at[layer, 0]),
            pltpu.make_async_copy(go_h.at[layer], go.at[layer], sem_q.at[layer, 1]),
            pltpu.make_async_copy(qr_h.at[layer], qr.at[layer], sem_q.at[layer, 2]),
        ]

    def w_copies(layer, step):
        part = pl.ds(step * HG, HG)
        return [
            pltpu.make_async_copy(wk_h.at[layer, part], wk.at[layer, part], sem_w.at[layer, step, 0]),
            pltpu.make_async_copy(wv_h.at[layer, part], wv.at[layer, part], sem_w.at[layer, step, 1]),
        ]

    keys = pltpu.make_async_copy(le_h, le, sem_q.at[layers, 0])
    keys.start()
    for layer in range(layers):
        for c in q_copies(layer):
            c.start()
        for step in range(steps):
            for c in w_copies(layer, step):
                c.start()

    acc[...] = jnp.zeros_like(acc)
    for s in range(2):
        t = me * tok + s * SUB + lax.broadcasted_iota(jnp.int32, (SUB, 128), 0)
        first = jnp.zeros((SUB, 128), jnp.int32)
        end = jnp.int32(0)
        for j in range(lens.shape[0]):
            end = end + lens[j]
            first = jnp.where(end <= t, end, first)
        for half in range(2):
            u = (
                me * tok - MARGIN + s * SUB + half * 128
                + lax.broadcasted_iota(jnp.int32, (SUB, 128), 1)
            )
            ok = (u >= first) & (u <= t)
            bias[s, :, half * 128 : half * 128 + 128] = jnp.where(ok, jnp.inf, -jnp.inf)
    keys.wait()
    low = lax.broadcasted_iota(jnp.int32, (SUB, 128), 1) < 64

    def layer_body(layer, carry):
        for c in q_copies(layer):
            c.wait()

        def widen(c, carry):
            part = pl.ds(pl.multiple_of(c * 512, 512), 512)
            qf[part, :] = qn[layer, part, :].astype(F32)
            gf[part, :] = go[layer, part, :].astype(F32)
            return carry

        lax.fori_loop(0, rows // 512, widen, 0)

        def step_body(step, carry):
            for c in w_copies(layer, step):
                c.wait()
            base = step * HG
            for i in range(HG):
                h = base + i
                qh = qf[pl.ds(h, tok, stride=heads), :].astype(BF)
                gh = gf[pl.ds(h, tok, stride=heads), :].astype(BF)
                a = dot(qh, wk[layer, h], 1, 0).astype(BF)
                b = dot(gh, wv[layer, h], 1, 1).astype(BF)
                lanes = pl.ds(pl.multiple_of((step * (HG // 2) + i // 2) * 128, 128), 128)
                for s in range(2):
                    mine = slice(i * SUB, i * SUB + SUB)
                    ql[s, mine, :lat] = a[s * SUB : s * SUB + SUB]
                    gl[s, mine, :] = b[s * SUB : s * SUB + SUB]
                    pair = qr[layer, s * SUB : s * SUB + SUB, lanes].astype(F32)
                    pair = jnp.where(low if i % 2 == 0 else ~low, pair, 0.0)
                    ql[s, mine, lat:] = pair.astype(BF)
            for s in range(2):
                win = slice(s * SUB, s * SUB + WIN)
                score = dot(ql[s], le[win, :], 1, 1) * scale
                score = jnp.minimum(score.reshape(HG, SUB, WIN), bias[s][None])
                score = score.reshape(HG * SUB, WIN)
                top = jnp.max(score, axis=1, keepdims=True)
                e = jnp.exp(score - top)
                prob = e * (1.0 / jnp.sum(e, axis=1, keepdims=True))
                dprob = dot(gl[s], le[win, :lat], 1, 1)
                delta = jnp.sum(prob * dprob, axis=1, keepdims=True)
                ds = (prob * (dprob - delta) * scale).astype(BF)
                low_p = prob.astype(BF)
                d = dot(ds, le[win, :], 1, 0)
                for i in range(HG):
                    dq[i, s * SUB : s * SUB + SUB, :] = d[i * SUB : i * SUB + SUB, :lat].astype(BF)
                for j in range(HG // 2):
                    even = d[2 * j * SUB : (2 * j + 1) * SUB, lat:]
                    odd = d[(2 * j + 1) * SUB : (2 * j + 2) * SUB, lat:]
                    lanes = pl.ds(pl.multiple_of((step * (HG // 2) + j) * 128, 128), 128)
                    ro[s * SUB : s * SUB + SUB, lanes] = jnp.where(low, even, odd).astype(BF)
                acc[win, :] += dot(ds, ql[s], 0, 0)
                acc[win, :lat] += dot(low_p, gl[s], 0, 0)
            for i in range(HG):
                h = base + i
                of[pl.ds(h, tok, stride=heads), :] = dot(dq[i], wk[layer, h], 1, 1)
            return carry

        lax.fori_loop(0, steps, step_body, 0)

        def place(k, carry):
            b = order[k]
            on[k, layer] = of[pl.ds(pl.multiple_of(b * (blk * heads), blk * heads), blk * heads), :].astype(BF)
            orp[k, layer] = ro[pl.ds(pl.multiple_of(b * blk, blk), blk), :]
            return carry

        lax.fori_loop(0, on.shape[0], place, 0)
        return carry

    lax.fori_loop(0, layers, layer_body, 0)


def call_attention(lens, order, qn, qr, go, le, wk, wv, groups):
    layers, rows, head = qn.shape
    tok, wide = qr.shape[1:]
    heads = rows // tok
    span, ext = le.shape
    lat = wk.shape[3]
    smem = pl.BlockSpec(memory_space=pltpu.SMEM)
    hbm = pl.BlockSpec(memory_space=pl.ANY)
    vmem = pl.BlockSpec(memory_space=pltpu.VMEM)
    return pl.pallas_call(
        attention,
        out_shape=(
            jax.ShapeDtypeStruct((groups, layers, rows // groups, head), BF),
            jax.ShapeDtypeStruct((groups, layers, tok // groups, wide), BF),
            jax.ShapeDtypeStruct((span, ext), F32),
        ),
        in_specs=[smem, smem] + [hbm] * 6,
        out_specs=(vmem, vmem, vmem),
        scratch_shapes=[
            pltpu.VMEM(qn.shape, BF),
            pltpu.VMEM(qr.shape, BF),
            pltpu.VMEM(go.shape, BF),
            pltpu.VMEM(le.shape, BF),
            pltpu.VMEM(wk.shape, BF),
            pltpu.VMEM(wv.shape, BF),
            pltpu.VMEM((rows, head), F32),
            pltpu.VMEM((rows, head), F32),
            pltpu.VMEM((rows, head), F32),
            pltpu.VMEM((tok, wide), BF),
            pltpu.VMEM((2, HG * SUB, ext), BF),
            pltpu.VMEM((2, HG * SUB, lat), BF),
            pltpu.VMEM((HG, tok, lat), BF),
            pltpu.VMEM((2, SUB, WIN), F32),
            pltpu.SemaphoreType.DMA((layers + 1, 3)),
            pltpu.SemaphoreType.DMA((layers, heads // HG, 2)),
        ],
        compiler_params=pltpu.CompilerParams(vmem_limit_bytes=60 * 1024 * 1024),
    )(lens, order, qn, qr, go, le, wk, wv)


def shift(value, by):
    n = lax.axis_size("cp")
    return lax.ppermute(value, "cp", [(i, (i + by) % n) for i in range(n)])


def on_device(q_nope, q_rope, grad_out, latent, key_rope, hidden_in, w_uk, w_uv, doc_lengths, plan):
    groups = lax.axis_size("cp")
    me = lax.axis_index("cp")
    layers, _, tok, heads, head = q_nope.shape
    lat = latent.shape[2]
    turned = key_rope[0].T
    own = jnp.concatenate([latent[0], turned, turned], axis=1)
    le = jnp.concatenate([shift(own[2 * tok - MARGIN :], 2), shift(own, 1), own], axis=0)
    on, orp, acc = call_attention(
        doc_lengths[0],
        plan[0][me],
        q_nope.reshape(layers, tok * heads, head),
        q_rope[:, 0],
        grad_out.reshape(layers, tok * heads, head),
        le,
        w_uk,
        w_uv,
        groups,
    )
    on = lax.all_to_all(on, "cp", split_axis=0, concat_axis=0, tiled=True)
    orp = lax.all_to_all(orp, "cp", split_axis=0, concat_axis=0, tiled=True)
    dq_nope = jnp.swapaxes(on, 0, 1).reshape(layers, 1, tok, heads, head)
    dq_rope = jnp.swapaxes(orp, 0, 1).reshape(q_rope.shape)
    part = jnp.concatenate([acc[:, :lat], acc[:, lat : lat + 64] + acc[:, lat + 64 :]], axis=1)
    edge = MARGIN - tok
    total = part[MARGIN:] + shift(part[edge:MARGIN], -1)
    total = total.at[tok - edge :].add(shift(part[:edge], -2))
    joined = total.astype(BF)
    d_latent = joined[:, :lat]
    rope_low = joined[:, lat:]
    cols = lax.all_to_all(hidden_in[0], "cp", split_axis=1, concat_axis=0, tiled=True)
    keys = lax.all_gather(joined, "cp", axis=0, tiled=True)
    d_wdkv = lax.psum_scatter(dot(cols, keys, 0, 0), "dp", scatter_dimension=0, tiled=True)
    return dq_nope, dq_rope, d_latent[None], rope_low.T[None], d_wdkv


def solution(mesh):
    placed = (
        P(None, "dp", "cp", None, None),
        P(None, "dp", "cp", None),
        P(None, "dp", "cp", None, None),
        P("dp", "cp", None),
        P("dp", None, "cp"),
        P("dp", "cp", None),
        P(),
        P(),
        P("dp", None),
        P("dp", None, None),
    )
    return jax.shard_map(
        on_device,
        mesh=mesh,
        in_specs=placed,
        out_specs=(
            P(None, "dp", "cp", None, None),
            P(None, "dp", "cp", None),
            P("dp", "cp", None),
            P("dp", None, "cp"),
            P(("cp", "dp"), None),
        ),
        check_vma=False,
    )
```

time: 699 us -> 226 us (0.32); the launches traced: 687 us -> 225 us
  matrix products: 337 us -> 4.64 us
  local copies, waits for them, and re-layouts: 118 us -> 13.9 us
  waiting for transfers between devices: 144 us -> 92.3 us
  Pallas kernels: 0 us -> 45 us
  other arithmetic: 26.6 us -> 4.67 us
  blocking collectives: 15.1 us -> 35.2 us
  loops' own time: 16.6 us -> 0 us
    dot_general x23 -> x1, matrix products: 337 us -> 4.64 us  [dot(): lax.dot_general(a, b, (((ca,), (cb,)), ((), ())), preferred_element_type=...]
    reduce_scatter x2 -> x0, waiting for transfers between devices: 61.2 us -> none  [the longest x1 34.4 us: on_device(): lax.psum_scatter(lat_total, 'cp', scatter_dimension=0, tiled=True)]
    pallas_call x0 -> x1, Pallas kernels: none -> 45 us  [call_attention(): pl.pallas_call(attention, out_shape=(jax.ShapeDtypeStruct((groups, layers...]
    gather x76 -> x0, local copies, waits for them, and re-layouts: 38.5 us -> none
    all_to_all x0 -> x1, blocking collectives: none -> 35.2 us  [on_device(): lax.all_to_all(hidden_in[0], 'cp', split_axis=1, concat_axis=0, tiled=True)]
    unnamed x5 -> x3, waiting for transfers between devices: 80.2 us -> 51.5 us
    all_to_all x3 -> x2, waiting for transfers between devices: 2.74 us -> 30.5 us  [the longest x1 22.7 us: on_device(): on = lax.all_to_all(on, 'cp', split_axis=0, concat_axis=0, tiled=True)]
    dynamic_update_slice x24 -> x0, local copies, waits for them, and re-layouts: 21.6 us -> none  [the longest x8 14.8 us: add_window(): lat_total = lax.dynamic_update_slice_in_dim(lat_total, piece, start, 0)]
  transfers between devices with their start and end apart: 7 -> 8, of which waited for: 4 -> 5; matrix products, arithmetic and copies ran while one was open for 33% -> 7% of each run, Pallas kernels for 0% -> 0%
where the time goes in v1:
time: 226 us; the launch traced here: 225 us
  waiting for transfers between devices  92.3 us (41%)
  Pallas kernels  45 us (20%)
  blocking collectives  35.2 us (16%)
  between operations  14.8 us (7%)
  starting transfers between devices  14.5 us (6%)
  local copies, waits for them, and re-layouts  13.9 us (6%)
  other arithmetic  4.67 us (2%)
  matrix products  4.64 us (2%)
    unnamed x3, waiting for transfers between devices  51.5 us
    pallas_call x1, Pallas kernels, call_attention(): pl.pallas_call(attention, out_shape=(jax.ShapeDtypeStruct((groups, layers...  45 us
    all_to_all x1, blocking collectives, on_device(): lax.all_to_all(hidden_in[0], 'cp', split_axis=1, concat_axis=0, tiled=True)  35.2 us
    all_to_all x1, waiting for transfers between devices, on_device(): on = lax.all_to_all(on, 'cp', split_axis=0, concat_axis=0, tiled=True)  22.7 us
    ppermute x4, waiting for transfers between devices, shift(): return lax.ppermute(value, 'cp', [(i, (i + by) % n) for i in range(n)])  10.4 us
    all_to_all x1, waiting for transfers between devices, on_device(): orp = lax.all_to_all(orp, 'cp', split_axis=0, concat_axis=0, tiled=True)  7.79 us
    unnamed x14, local copies, waits for them, and re-layouts  6.46 us
    ppermute x4, starting transfers between devices, shift(): return lax.ppermute(value, 'cp', [(i, (i + by) % n) for i in range(n)])  5.33 us
  transfers between devices with their start and end apart: 8, of which 5 were waited for; matrix products, arithmetic and copies ran while one was open for 7% of the time, Pallas kernels for 0%

profile of v1, /device:TPU:1, one launch (start us, length us, event | category | flops | bytes accessed | tf_op | source)
XLA Modules:
  0.0 225.1 jit_solution(15688939413656299971)
XLA Ops:
  7.2 0.0 copy-start
  7.2 0.0 all-gather.2.cloned.1.call-start
  7.2 0.8 copy.34
  8.1 1.0 pad_maximum_fusion.1
  9.1 2.6 %collective-permute-start.1 = (bf16[128,640]{1,0:T(8,128)(2,1)S(1)}, bf16[128,640]{1,0:T(8,128)(2,1)S(1)}, u32[]{:S(2)}, u32[]{:S(2)}) collective-permute-start(bf16[128,640]{1,0:T(8,128)(2,1)S(1)} %pad_maximum_fusion.1), channel_id=1, source_target_pairs={{0,16},{16,32},{32,48},{48,64},{64,80},{80,96},{96,112},{112,0},{1... | collective-permute-start | bytes 491528 | tf_op jit(solution)/shard_map/ppermute | solution.py:191
  11.7 1.3 collective-permute-start
  13.0 0.0 copy-done
  13.0 0.5 dynamic-slice_bitcast_fusion.order
  13.5 4.0 %collective-permute-done = bf16[64,640]{1,0:T(8,128)(2,1)S(1)} collective-permute-done((bf16[64,640]{1,0:T(8,128)(2,1)S(1)}, bf16[64,640]{1,0:T(8,128)(2,1)S(1)}, u32[]{:S(2)}, u32[]{:S(2)}) %collective-permute-start) | collective-permute-done | bytes 81952 | tf_op jit(solution)/shard_map/ppermute | solution.py:191
  17.5 0.0 collective-permute-done.1
  17.5 1.8 maximum_maximum_fusion.le_h
  19.3 45.0 %shard_map.137 = (bf16[8,2,512,128]{3,2,1,0:T(8,128)(2,1)}, bf16[8,2,16,2048]{3,2,1,0:T(8,128)(2,1)}, f32[320,640]{1,0:T(8,128)}) custom-call(s32[32]{0:T(128)} %bitcast.48, s32[8]{0:T(128)} %dynamic-slice_bitcast_fusion.order, bf16[2,4096,128]{2,1,0:T(8,128)(2,1)} %bitcast.39, bf16[2,128,2048]{2,1,0:T(8,128)(2,1)} %bitcast.42, ...), custom_call_target="tpu_custom_call" | custom-call | tf_op jit(solution)/shard_map/pallas_call | solution.py:158
  64.3 1.1 slice.47
  65.5 1.1 slice_add_fusion.1
  66.6 0.0 copy-start.1
  66.6 0.0 collective-permute-start.2
  66.7 1.4 collective-permute-start.3
  68.1 6.3 %collective-permute-done.2 = f32[128,576]{1,0:T(8,128)S(1)} collective-permute-done((f32[128,576]{1,0:T(8,128)S(1)}, f32[128,576]{1,0:T(8,128)S(1)}, u32[]{:S(2)}, u32[]{:S(2)}) %collective-permute-start.2) | collective-permute-done | bytes 294944 | tf_op jit(solution)/shard_map/ppermute | solution.py:191
  74.4 0.0 collective-permute-done.3
  74.5 0.7 convert_element_type.3
  75.2 0.0 all-gather.2.cloned.1.call-update
  75.2 0.0 copy-done.1
  75.2 2.3 %copy.37 = bf16[1,128,7168]{1,2,0:T(8,128)(2,1)} copy(bf16[1,128,7168]{2,1,0:T(8,128)(2,1)S(1)} %copy-done.1) | data formatting | bytes 3670016 | tf_op args[5]
  77.6 35.2 %all_to_all.29 = bf16[128,8,896]{0,2,1:T(8,128)(2,1)S(1)} all-to-all(bf16[128,8,896]{0,2,1:T(8,128)(2,1)} %bitcast.36), channel_id=1, replica_groups=mesh['cp'=8,'dp'=16] {'cp'}, dimensions={1} | all-to-all | bytes 3670016 | tf_op jit(solution)/shard_map/all_to_all | solution.py:224
  112.8 4.5 %all-to-all-start.1 = ((bf16[8,2,16,2048]{3,2,1,0:T(8,128)(2,1)}), bf16[8,2,16,2048]{3,2,1,0:T(8,128)(2,1)S(1)}, u32[]{:S(2)}, u32[]{:S(2)}) async-start(bf16[8,2,16,2048]{3,2,1,0:T(8,128)(2,1)} %get-tuple-element.21), calls=%async_computation.1 | async-start | bytes 2097152 | tf_op jit(solution)/shard_map/all_to_all | solution.py:214
  117.3 0.0 all-reduce.3.cloned.1.call-start
  117.3 2.7 %copy.38 = bf16[8,128,896]{2,1,0:T(8,128)(2,1)} copy(bf16[8,128,896]{1,2,0:T(8,128)(2,1)S(1)} %bitcast.35) | data formatting | bytes 3670016 | tf_op jit(solution)/shard_map/all_to_all | solution.py:224
  120.0 0.0 all-gather.2.cloned.1.call-done
  120.0 4.6 %convolution_bitcast_fusion = f32[896,576]{0,1:T(8,128)} fusion(bf16[1024,576]{1,0:T(8,128)(2,1)} %all-gather.2.cloned.1.call-done, bf16[1024,896]{1,0:T(8,128)(2,1)} %bitcast.37), kind=kOutput, calls=%fused_computation | convolution fusion | flops 1056964608 | bytes 5079040 | tf_op jit(solution)/shard_map/dot_general | solution.py:20
  124.6 0.0 all-reduce.3.cloned.1.call-update
  124.6 7.8 %all-to-all-done.1 = bf16[8,2,16,2048]{3,2,1,0:T(8,128)(2,1)S(1)} async-done(((bf16[8,2,16,2048]{3,2,1,0:T(8,128)(2,1)}), bf16[8,2,16,2048]{3,2,1,0:T(8,128)(2,1)S(1)}, u32[]{:S(2)}, u32[]{:S(2)}) %all-to-all-start.1) | async-done | bytes 1048608 | tf_op jit(solution)/shard_map/all_to_all | solution.py:214
  132.4 0.0 copy-start.3
  132.4 0.0 copy-start.2
  132.4 4.6 %all-to-all-start = ((bf16[8,2,512,128]{3,2,1,0:T(8,128)(2,1)}), bf16[8,2,512,128]{3,2,1,0:T(8,128)(2,1)S(1)}, u32[]{:S(2)}, u32[]{:S(2)}) async-start(bf16[8,2,512,128]{3,2,1,0:T(8,128)(2,1)} %get-tuple-element.20), calls=%async_computation | async-start | bytes 4194304 | tf_op jit(solution)/shard_map/all_to_all | solution.py:213
  137.0 0.0 copy-done.3
  137.0 0.6 dynamic-slice.9
  138.2 0.0 copy-done.2
  138.3 0.7 copy.41
  139.0 0.7 slice_bitcast_fusion
  139.6 1.0 copy.36
  140.7 22.7 %all-to-all-done = bf16[8,2,512,128]{3,2,1,0:T(8,128)(2,1)S(1)} async-done(((bf16[8,2,512,128]{3,2,1,0:T(8,128)(2,1)}), bf16[8,2,512,128]{3,2,1,0:T(8,128)(2,1)S(1)}, u32[]{:S(2)}, u32[]{:S(2)}) %all-to-all-start) | async-done | bytes 2097184 | tf_op jit(solution)/shard_map/all_to_all | solution.py:213
  163.4 1.5 copy.35
  164.8 51.4 %all-reduce.3.cloned.1.call-done = f32[896,576]{0,1:T(8,128)} async-done(((f32[896,576]{0,1:T(8,128)}), f32[896,576]{0,1:T(8,128)}) %all-reduce.3.cloned.1.call-update) | async-done | bytes 2064400
  216.3 1.2 constant_dynamic-slice_fusion
  217.5 0.8 copy.42
  (6 shorter events, 0.1 us)
Async XLA Ops:
  7.2 5.8 %copy-start = (s32[1,8,8]{2,1,0:T(8,128)S(1)}, s32[1,8,8]{2,1,0:T(8,128)}, u32[]{:S(2)}) copy-start(s32[1,8,8]{2,1,0:T(8,128)} %param.21) | copy-start | bytes 772
  7.2 112.8 %all-gather.2.cloned.1.call-start = ((), (), s32[]{:S(2)}) async-start(), calls=%async_computation.3 | async-start | bytes 1474560 | tf_op jit(solution)/shard_map/all_gather | solution.py:225
  9.1 8.5 %collective-permute-start.1 = (bf16[128,640]{1,0:T(8,128)(2,1)S(1)}, bf16[128,640]{1,0:T(8,128)(2,1)S(1)}, u32[]{:S(2)}, u32[]{:S(2)}) collective-permute-start(bf16[128,640]{1,0:T(8,128)(2,1)S(1)} %pad_maximum_fusion.1), channel_id=1, source_target_pairs={{0,16},{16,32},{32,48},{48,64},{64,80},{80,96},{96,112},{112,0},{1... | collective-permute-start | bytes 491528 | tf_op jit(solution)/shard_map/ppermute | solution.py:191
  11.7 5.8 %collective-permute-start = (bf16[64,640]{1,0:T(8,128)(2,1)S(1)}, bf16[64,640]{1,0:T(8,128)(2,1)S(1)}, u32[]{:S(2)}, u32[]{:S(2)}) collective-permute-start(bf16[64,640]{1,0:T(8,128)(2,1)S(1)} %slice.56), channel_id=1, source_target_pairs={{0,32},{16,48},{32,64},{48,80},{64,96},{80,112},{96,0},{112,16},{1... | collective-permute-start | bytes 245768 | tf_op jit(solution)/shard_map/ppermute | solution.py:191
  66.6 8.6 %copy-start.1 = (bf16[1,128,7168]{2,1,0:T(8,128)(2,1)S(1)}, bf16[1,128,7168]{2,1,0:T(8,128)(2,1)}, u32[]{:S(2)}) copy-start(bf16[1,128,7168]{2,1,0:T(8,128)(2,1)} %param.17) | copy-start | bytes 5505028
  66.6 7.8 %collective-permute-start.2 = (f32[128,576]{1,0:T(8,128)S(1)}, f32[128,576]{1,0:T(8,128)S(1)}, u32[]{:S(2)}, u32[]{:S(2)}) collective-permute-start(f32[128,576]{1,0:T(8,128)S(1)} %fusion), channel_id=1, source_target_pairs={{0,112},{16,0},{32,16},{48,32},{64,48},{80,64},{96,80},{112,96},{1... | collective-permute-start | bytes 884744 | tf_op jit(solution)/shard_map/ppermute | solution.py:191
  66.7 7.8 %collective-permute-start.3 = (f32[64,576]{1,0:T(8,128)S(1)}, f32[64,576]{1,0:T(8,128)S(1)}, u32[]{:S(2)}, u32[]{:S(2)}) collective-permute-start(f32[64,576]{1,0:T(8,128)S(1)} %pad_maximum_fusion), channel_id=1, source_target_pairs={{0,96},{16,112},{32,0},{48,16},{64,32},{80,48},{96,64},{112,80},{1... | collective-permute-start | bytes 442376 | tf_op jit(solution)/shard_map/ppermute | solution.py:191
  112.8 19.6 %all-to-all-start.1 = ((bf16[8,2,16,2048]{3,2,1,0:T(8,128)(2,1)}), bf16[8,2,16,2048]{3,2,1,0:T(8,128)(2,1)S(1)}, u32[]{:S(2)}, u32[]{:S(2)}) async-start(bf16[8,2,16,2048]{3,2,1,0:T(8,128)(2,1)} %get-tuple-element.21), calls=%async_computation.1 | async-start | bytes 2097152 | tf_op jit(solution)/shard_map/all_to_all | solution.py:214
  117.3 99.0 %all-reduce.3.cloned.1.call-start = ((), (), s32[]{:S(2)}) async-start(), calls=%async_computation.4 | async-start | bytes 4128768
  132.4 4.6 %copy-start.3 = (u32[128]{0:T(128)S(1)}, u32[128]{0:T(128)}, u32[]{:S(2)}) copy-start(u32[128]{0:T(128)} %constant.49) | copy-start | bytes 1540
  132.4 5.8 %copy-start.2 = (bf16[128,576]{1,0:T(8,128)(2,1)S(1)}, bf16[128,576]{1,0:T(8,128)(2,1)}, u32[]{:S(2)}) copy-start(bf16[128,576]{1,0:T(8,128)(2,1)} %convert_element_type.3) | copy-start | bytes 442372
  132.4 30.9 %all-to-all-start = ((bf16[8,2,512,128]{3,2,1,0:T(8,128)(2,1)}), bf16[8,2,512,128]{3,2,1,0:T(8,128)(2,1)S(1)}, u32[]{:S(2)}, u32[]{:S(2)}) async-start(bf16[8,2,512,128]{3,2,1,0:T(8,128)(2,1)} %get-tuple-element.20), calls=%async_computation | async-start | bytes 4194304 | tf_op jit(solution)/shard_map/all_to_all | solution.py:213
Sparse Core Ops, SparseCore 0:
  75.4 35.4 all-gather.1
  124.7 91.4 all-reduce.2

commit v2 on v1

v2 whole, which is shorter than its diff:
```python
import functools
import math

import jax
import jax.numpy as jnp
from jax import lax
from jax.experimental import pallas as pl
from jax.experimental.pallas import tpu as pltpu
from jax.sharding import PartitionSpec as P

BF = jnp.bfloat16
F32 = jnp.float32
MESH = pl.DeviceIdType.MESH
MARGIN = 192
SUB = 64
WIN = 256
HG = 8
ROPE = 64
PIECE = 64


def dot(a, b, ca, cb):
    return lax.dot_general(a, b, (((ca,), (cb,)), ((), ())), preferred_element_type=F32)


def each(count, body):
    def step(i, carry):
        body(i)
        return carry

    lax.fori_loop(0, count, step, 0)


def kernel(
    ncp, ndp, side,
    lens, plan, qn_h, qr_h, go_h, lat_h, kr_h, hid_h, wk_h, wv_h,
    dqn_h, dqr_h, dlat, dkr, dw,
    qn, qr, go, le, kr, hid, wk, wv, qf, gf, of, ro, ql, gl, dq, bias, acc, on, orp,
    slab, ht, hr, back, back1, back2, joined, jr, part, parts,
    sem_q, sem_w, sem_k, sem_halo, sem_hs, sem_hr, sem_os, sem_or, sem_back,
    sem_near, sem_fwd_s, sem_fwd_r, sem_ps, sem_pr, sem_own,
):
    layers, rows, head = qn.shape
    tok = qr.shape[1]
    heads = rows // tok
    lat = gl.shape[2]
    ext = le.shape[1]
    steps = heads // HG
    blk = tok // ncp
    scale = 1.0 / math.sqrt(head + ROPE)
    c_me = lax.axis_index("cp")
    d_me = lax.axis_index("dp")

    def cp_dev(offset):
        return lax.rem(c_me + offset + ncp, ncp)

    def dp_dev(offset):
        return lax.rem(d_me + offset + ndp, ndp)

    def q_copies(layer):
        return [
            pltpu.make_async_copy(qn_h.at[layer], qn.at[layer], sem_q.at[layer, 0]),
            pltpu.make_async_copy(go_h.at[layer], go.at[layer], sem_q.at[layer, 1]),
            pltpu.make_async_copy(qr_h.at[layer], qr.at[layer], sem_q.at[layer, 2]),
        ]

    def w_copies(layer, step):
        heads_of = pl.ds(step * HG, HG)
        return [
            pltpu.make_async_copy(wk_h.at[layer, heads_of], wk.at[layer, heads_of], sem_w.at[layer, step, 0]),
            pltpu.make_async_copy(wv_h.at[layer, heads_of], wv.at[layer, heads_of], sem_w.at[layer, step, 1]),
        ]

    own_rows = slice(MARGIN, MARGIN + tok)
    edge = MARGIN - tok
    k_copies = [
        pltpu.make_async_copy(lat_h, le.at[own_rows, :lat], sem_k.at[0]),
        pltpu.make_async_copy(kr_h, kr, sem_k.at[1]),
        pltpu.make_async_copy(hid_h, hid, sem_k.at[2]),
    ]
    for c in k_copies:
        c.start()
    for layer in range(layers):
        for c in q_copies(layer):
            c.start()
        for step in range(steps):
            for c in w_copies(layer, step):
                c.start()

    barrier = pltpu.get_barrier_semaphore()

    def greet_cp(i):
        pl.semaphore_signal(barrier, inc=1, device_id=(cp_dev(i + 1), d_me), device_id_type=MESH)

    def greet_dp(i):
        pl.semaphore_signal(barrier, inc=1, device_id=(c_me, dp_dev(i + 1)), device_id_type=MESH)

    each(ncp - 1, greet_cp)
    each(ndp - 1, greet_dp)

    k_copies[0].wait()
    k_copies[1].wait()
    turned = kr[...].astype(F32)
    le[own_rows, lat:] = jnp.concatenate([turned, turned], axis=0).T.astype(BF)
    pl.semaphore_wait(barrier, ncp + ndp - 2)

    halo = [
        pltpu.make_async_remote_copy(
            le.at[own_rows], le.at[edge:MARGIN], sem_halo.at[0], sem_halo.at[1],
            device_id=(cp_dev(1), d_me), device_id_type=MESH,
        ),
        pltpu.make_async_remote_copy(
            le.at[MARGIN + tok - edge : MARGIN + tok], le.at[:edge], sem_halo.at[2], sem_halo.at[3],
            device_id=(cp_dev(2), d_me), device_id_type=MESH,
        ),
    ]
    for c in halo:
        c.start()

    k_copies[2].wait()
    width = hid.shape[1] // ncp
    rows_dev = width // ndp

    def turn(c):
        for j in range(width // 128):
            lanes = pl.ds(pl.multiple_of(c * width + j * 128, 128), 128)
            slab[j * 128 : j * 128 + 128, :] = hid[:, lanes].astype(F32).T
        pad = jnp.zeros((PIECE - rows_dev, tok), F32)
        for j in range(ndp):
            piece = jnp.concatenate([slab[j * rows_dev : (j + 1) * rows_dev, :], pad], axis=0)
            ht[j, pl.ds(pl.multiple_of(c * PIECE, PIECE), PIECE), :] = piece.astype(BF)

    each(ncp, turn)

    def my_lanes():
        return pl.ds(pl.multiple_of(d_me * tok, tok), tok)

    def hidden_copy(i):
        to = dp_dev(i + 1)
        return pltpu.make_async_remote_copy(
            ht.at[to], hr.at[:, my_lanes()], sem_hs.at[i], sem_hr.at[i],
            device_id=(c_me, to), device_id_type=MESH,
        )

    each(ndp - 1, lambda i: hidden_copy(i).start())
    hidden_own = pltpu.make_async_copy(ht.at[d_me], hr.at[:, my_lanes()], sem_own.at[0])
    hidden_own.start()

    acc[...] = jnp.zeros_like(acc)
    for s in range(2):
        t = c_me * tok + s * SUB + lax.broadcasted_iota(jnp.int32, (SUB, 128), 0)
        first = jnp.zeros((SUB, 128), jnp.int32)
        end = jnp.int32(0)
        for j in range(lens.shape[1]):
            end = end + lens[0, j]
            first = jnp.where(end <= t, end, first)
        for half in range(2):
            u = (
                c_me * tok - MARGIN + s * SUB + half * 128
                + lax.broadcasted_iota(jnp.int32, (SUB, 128), 1)
            )
            ok = (u >= first) & (u <= t)
            bias[s, :, half * 128 : half * 128 + 128] = jnp.where(ok, jnp.inf, -jnp.inf)
    low = lax.broadcasted_iota(jnp.int32, (SUB, 128), 1) < ROPE
    for c in halo:
        c.wait_recv()

    def out_copies(layer, i):
        to = cp_dev(i + 1)
        return [
            pltpu.make_async_remote_copy(
                on.at[to, layer],
                dqn_h.at[layer, pl.ds(pl.multiple_of(c_me * (blk * heads), blk * heads), blk * heads)],
                sem_os.at[layer, i, 0], sem_or.at[layer, i, 0],
                device_id=(to, d_me), device_id_type=MESH,
            ),
            pltpu.make_async_remote_copy(
                orp.at[to, layer],
                dqr_h.at[layer, pl.ds(pl.multiple_of(c_me * blk, blk), blk)],
                sem_os.at[layer, i, 1], sem_or.at[layer, i, 1],
                device_id=(to, d_me), device_id_type=MESH,
            ),
        ]

    def out_own(layer):
        return [
            pltpu.make_async_copy(
                on.at[c_me, layer],
                dqn_h.at[layer, pl.ds(pl.multiple_of(c_me * (blk * heads), blk * heads), blk * heads)],
                sem_own.at[1 + 2 * layer],
            ),
            pltpu.make_async_copy(
                orp.at[c_me, layer],
                dqr_h.at[layer, pl.ds(pl.multiple_of(c_me * blk, blk), blk)],
                sem_own.at[2 + 2 * layer],
            ),
        ]

    def compute(layer):
        for c in q_copies(layer):
            c.wait()

        def widen(c):
            chunk = pl.ds(pl.multiple_of(c * 512, 512), 512)
            qf[chunk, :] = qn[layer, chunk, :].astype(F32)
            gf[chunk, :] = go[layer, chunk, :].astype(F32)

        each(rows // 512, widen)

        def step_body(step):
            for c in w_copies(layer, step):
                c.wait()
            base = step * HG
            for i in range(HG):
                h = base + i
                qh = qf[pl.ds(h, tok, stride=heads), :].astype(BF)
                gh = gf[pl.ds(h, tok, stride=heads), :].astype(BF)
                a = dot(qh, wk[layer, h], 1, 0).astype(BF)
                b = dot(gh, wv[layer, h], 1, 1).astype(BF)
                lanes = pl.ds(pl.multiple_of((step * (HG // 2) + i // 2) * 128, 128), 128)
                for s in range(2):
                    mine = slice(i * SUB, i * SUB + SUB)
                    ql[s, mine, :lat] = a[s * SUB : s * SUB + SUB]
                    gl[s, mine, :] = b[s * SUB : s * SUB + SUB]
                    pair = qr[layer, s * SUB : s * SUB + SUB, lanes].astype(F32)
                    pair = jnp.where(low if i % 2 == 0 else ~low, pair, 0.0)
                    ql[s, mine, lat:] = pair.astype(BF)
            for s in range(2):
                win = slice(s * SUB, s * SUB + WIN)
                score = dot(ql[s], le[win, :], 1, 1) * scale
                score = jnp.minimum(score.reshape(HG, SUB, WIN), bias[s][None])
                score = score.reshape(HG * SUB, WIN)
                top = jnp.max(score, axis=1, keepdims=True)
                e = jnp.exp(score - top)
                prob = e * (1.0 / jnp.sum(e, axis=1, keepdims=True))
                dprob = dot(gl[s], le[win, :lat], 1, 1)
                delta = jnp.sum(prob * dprob, axis=1, keepdims=True)
                ds = (prob * (dprob - delta) * scale).astype(BF)
                low_p = prob.astype(BF)
                d = dot(ds, le[win, :], 1, 0)
                for i in range(HG):
                    dq[i, s * SUB : s * SUB + SUB, :] = d[i * SUB : i * SUB + SUB, :lat].astype(BF)
                for j in range(HG // 2):
                    even = d[2 * j * SUB : (2 * j + 1) * SUB, lat:]
                    odd = d[(2 * j + 1) * SUB : (2 * j + 2) * SUB, lat:]
                    lanes = pl.ds(pl.multiple_of((step * (HG // 2) + j) * 128, 128), 128)
                    both = jnp.where(low, even, odd).astype(BF)
                    for q in range(SUB // blk):
                        ro[s * (SUB // blk) + q, :, lanes] = both[q * blk : q * blk + blk]
                acc[win, :] += dot(ds, ql[s], 0, 0)
                acc[win, :lat] += dot(low_p, gl[s], 0, 0)
            for i in range(HG):
                h = base + i
                back_q = dot(dq[i], wk[layer, h], 1, 1)
                for q in range(ncp):
                    of[q, pl.ds(h, blk, stride=heads), :] = back_q[q * blk : q * blk + blk]

        each(steps, step_body)

    def send_out(layer):
        def place(k):
            b = plan[0, c_me, k]
            on[k, layer] = of[b].astype(BF)
            orp[k, layer] = ro[b]

        each(ncp, place)

        def start(i):
            for c in out_copies(layer, i):
                c.start()

        each(ncp - 1, start)
        for c in out_own(layer):
            c.start()

    back_copies = [
        pltpu.make_async_remote_copy(
            back.at[edge:MARGIN], back1, sem_back.at[0], sem_back.at[1],
            device_id=(cp_dev(-1), d_me), device_id_type=MESH,
        ),
        pltpu.make_async_remote_copy(
            back.at[:edge], back2, sem_back.at[2], sem_back.at[3],
            device_id=(cp_dev(-2), d_me), device_id_type=MESH,
        ),
    ]

    def run_layer(layer):
        compute(layer)

        @pl.when(layer == layers - 1)
        def _():
            back[...] = acc[:MARGIN, :].astype(BF)
            for c in back_copies:
                c.start()

        send_out(layer)

    each(layers, run_layer)

    for c in back_copies:
        c.wait_recv()
    total = acc[own_rows, :] + back1[...].astype(F32)
    late = total[tok - edge :] + back2[...].astype(F32)
    total = jnp.concatenate([total[: tok - edge], late], axis=0)
    rope = total[:, lat:]
    rope = rope + pltpu.roll(rope, ROPE, 1)
    low_all = lax.broadcasted_iota(jnp.int32, (tok, 128), 1) < ROPE
    rope = jnp.where(low_all, rope, 0.0)
    joined[:, :lat] = total[:, :lat].astype(BF)
    joined[:, lat:] = rope.astype(BF)
    dlat[...] = total[:, :lat].astype(BF)
    dkr[...] = rope.T[:ROPE].astype(BF)

    y, z = d_me // side, lax.rem(d_me, side)
    other = ndp // side
    half = tok // 2

    def place_of(yy, zz, which):
        return jr.at[pl.ds(pl.multiple_of((yy * side + zz) * tok + which * half, half), half)]

    def ring(value, offset, n):
        return lax.rem(value + offset + n, n)

    def near(which, k):
        src = joined.at[which * half : which * half + half]
        to = y * side + ring(z, k, side) if which == 0 else ring(y, k, other) * side + z
        return pltpu.make_async_remote_copy(
            src, place_of(y, z, which), sem_near.at[which, 0, k - 1], sem_near.at[which, 1, k - 1],
            device_id=(c_me, to), device_id_type=MESH,
        )

    def forward(which, j, k):
        if which == 0:
            ref = place_of(y, ring(z, -j, side), 0)
            to = ring(y, k, other) * side + z
        else:
            ref = place_of(ring(y, -j, other), z, 1)
            to = y * side + ring(z, k, side)
        src = joined.at[which * half : which * half + half] if j == 0 else ref
        return pltpu.make_async_remote_copy(
            src, ref, sem_fwd_s.at[which, j, k - 1], sem_fwd_r.at[which, j, k - 1],
            device_id=(c_me, to), device_id_type=MESH,
        )

    for k in (1, 3, 2):
        near(0, k).start()
        near(1, k).start()
    for k in (1, 3, 2):
        forward(0, 0, k).start()
        forward(1, 0, k).start()
    gather_own = pltpu.make_async_copy(
        joined, jr.at[pl.ds(pl.multiple_of(d_me * tok, tok), tok)], sem_own.at[0]
    )
    hidden_own.wait()
    gather_own.start()
    for j in (1, 3, 2):
        for which in range(2):
            near(which, j).wait_recv()
            for k in (1, 3, 2):
                forward(which, j, k).start()
    each(ndp - 1, lambda i: hidden_copy(i).wait())
    gather_own.wait()
    for j in range(4):
        for which in range(2):
            for k in (1, 2, 3):
                forward(which, j, k).wait_recv()

    def product(c):
        piece = pl.ds(pl.multiple_of(c * 128, 128), 128)
        part[piece, :] = dot(hr[piece, :], jr[...], 1, 0).astype(BF)

    each(part.shape[0] // 128, product)

    def part_copy(i):
        to = cp_dev(i + 1)
        return pltpu.make_async_remote_copy(
            part.at[pl.ds(pl.multiple_of(to * PIECE, PIECE), PIECE)], parts.at[i],
            sem_ps.at[i], sem_pr.at[i], device_id=(to, d_me), device_id_type=MESH,
        )

    each(ncp - 1, lambda i: part_copy(i).start())
    mine = part[pl.ds(pl.multiple_of(c_me * PIECE, PIECE), PIECE), :].astype(F32)
    for i in range(ncp - 1):
        part_copy(i).wait_recv()
        mine = mine + parts[i].astype(F32)
    dw[...] = mine[:rows_dev, : lat + ROPE]

    for c in halo + back_copies:
        c.wait_send()
    for which in range(2):
        for k in (1, 2, 3):
            near(which, k).wait_send()
        for j in range(4):
            for k in (1, 2, 3):
                forward(which, j, k).wait_send()
    each(ncp - 1, lambda i: part_copy(i).wait_send())
    for layer in range(layers):
        for c in out_own(layer):
            c.wait()

        def finish(i):
            for c in out_copies(layer, i):
                c.wait()

        each(ncp - 1, finish)


def on_device(q_nope, q_rope, grad_out, latent, key_rope, hidden_in, w_uk, w_uv, doc_lengths, plan):
    ncp = lax.axis_size("cp")
    ndp = lax.axis_size("dp")
    side = math.isqrt(ndp)
    layers, _, tok, heads, head = q_nope.shape
    wide = q_rope.shape[3]
    lat = latent.shape[2]
    model = hidden_in.shape[2]
    ext = lat + 2 * ROPE
    rows = tok * heads
    smem = pl.BlockSpec(memory_space=pltpu.SMEM)
    hbm = pl.BlockSpec(memory_space=pl.ANY)
    vmem = pl.BlockSpec(memory_space=pltpu.VMEM)
    dma = pltpu.SemaphoreType.DMA
    dqn, dqr, dlat, dkr, dw = pl.pallas_call(
        functools.partial(kernel, ncp, ndp, side),
        out_shape=(
            jax.ShapeDtypeStruct((layers, rows, head), BF),
            jax.ShapeDtypeStruct((layers, tok, wide), BF),
            jax.ShapeDtypeStruct((tok, lat), BF),
            jax.ShapeDtypeStruct((ROPE, tok), BF),
            jax.ShapeDtypeStruct((model // (ncp * ndp), lat + ROPE), F32),
        ),
        in_specs=[smem, smem] + [hbm] * 8,
        out_specs=(hbm, hbm, vmem, vmem, vmem),
        scratch_shapes=[
            pltpu.VMEM((layers, rows, head), BF),
            pltpu.VMEM((layers, tok, wide), BF),
            pltpu.VMEM((layers, rows, head), BF),
            pltpu.VMEM((MARGIN + tok, ext), BF),
            pltpu.VMEM((ROPE, tok), BF),
            pltpu.VMEM((tok, model), BF),
            pltpu.VMEM(w_uk.shape, BF),
            pltpu.VMEM(w_uv.shape, BF),
            pltpu.VMEM((rows, head), F32),
            pltpu.VMEM((rows, head), F32),
            pltpu.VMEM((ncp, rows // ncp, head), F32),
            pltpu.VMEM((ncp, tok // ncp, wide), BF),
            pltpu.VMEM((2, HG * SUB, ext), BF),
            pltpu.VMEM((2, HG * SUB, lat), BF),
            pltpu.VMEM((HG, tok, lat), BF),
            pltpu.VMEM((2, SUB, WIN), F32),
            pltpu.VMEM((MARGIN + tok, ext), F32),
            pltpu.VMEM((ncp, layers, rows // ncp, head), BF),
            pltpu.VMEM((ncp, layers, tok // ncp, wide), BF),
            pltpu.VMEM((model // ncp, tok), F32),
            pltpu.VMEM((ndp, ncp * PIECE, tok), BF),
            pltpu.VMEM((ncp * PIECE, ndp * tok), BF),
            pltpu.VMEM((MARGIN, ext), BF),
            pltpu.VMEM((tok, ext), BF),
            pltpu.VMEM((MARGIN - tok, ext), BF),
            pltpu.VMEM((tok, ext), BF),
            pltpu.VMEM((ndp * tok, ext), BF),
            pltpu.VMEM((ncp * PIECE, ext), BF),
            pltpu.VMEM((ncp - 1, PIECE, ext), BF),
            dma((layers, 3)),
            dma((layers, heads // HG, 2)),
            dma((3,)),
            dma((4,)),
            dma((ndp - 1,)),
            dma((ndp - 1,)),
            dma((layers, ncp - 1, 2)),
            dma((layers, ncp - 1, 2)),
            dma((4,)),
            dma((2, 2, 3)),
            dma((2, 4, 3)),
            dma((2, 4, 3)),
            dma((ncp - 1,)),
            dma((ncp - 1,)),
            dma((1 + 2 * layers,)),
        ],
        compiler_params=pltpu.CompilerParams(
            collective_id=0, has_side_effects=True, vmem_limit_bytes=60 * 1024 * 1024
        ),
        name="attention_backward",
    )(
        doc_lengths,
        plan,
        q_nope.reshape(layers, rows, head),
        q_rope[:, 0],
        grad_out.reshape(layers, rows, head),
        latent[0],
        key_rope[0],
        hidden_in[0],
        w_uk,
        w_uv,
    )
    return (
        dqn.reshape(q_nope.shape),
        dqr.reshape(q_rope.shape),
        dlat[None],
        dkr[None],
        dw,
    )


def solution(mesh):
    placed = (
        P(None, "dp", "cp", None, None),
        P(None, "dp", "cp", None),
        P(None, "dp", "cp", None, None),
        P("dp", "cp", None),
        P("dp", None, "cp"),
        P("dp", "cp", None),
        P(),
        P(),
        P("dp", None),
        P("dp", None, None),
    )
    return jax.shard_map(
        on_device,
        mesh=mesh,
        in_specs=placed,
        out_specs=(
            P(None, "dp", "cp", None, None),
            P(None, "dp", "cp", None),
            P("dp", "cp", None),
            P("dp", None, "cp"),
            P(("cp", "dp"), None),
        ),
        check_vma=False,
    )
```

time: 226 us -> 105 us (0.46)
  waiting for transfers between devices: 92.3 us -> 0 us
  Pallas kernels: 45 us -> 98 us
  blocking collectives: 35.2 us -> 0 us
  starting transfers between devices: 14.5 us -> 0 us
  between operations: 14.8 us -> 0.66 us
  local copies, waits for them, and re-layouts: 13.9 us -> 6.28 us
  other arithmetic: 4.67 us -> 0 us
  matrix products: 4.64 us -> 0 us
    pallas_call x1, Pallas kernels: 45 us -> 98 us  [on_device(): pl.pallas_call(functools.partial(kernel, ncp, ndp, side), out_shape=(jax....]
    unnamed x3 -> x0, waiting for transfers between devices: 51.5 us -> none
    all_to_all x1 -> x0, blocking collectives: 35.2 us -> none  [on_device(): lax.all_to_all(hidden_in[0], 'cp', split_axis=1, concat_axis=0, tiled=True)]
    all_to_all x2 -> x0, waiting for transfers between devices: 30.5 us -> none  [the longest x1 22.7 us: on_device(): on = lax.all_to_all(on, 'cp', split_axis=0, concat_axis=0, tiled=True)]
    ppermute x4 -> x0, waiting for transfers between devices: 10.4 us -> none  [shift(): return lax.ppermute(value, 'cp', [(i, (i + by) % n) for i in range(n)])]
    all_to_all x2 -> x0, starting transfers between devices: 9.09 us -> none  [the longest x1 4.59 us: on_device(): on = lax.all_to_all(on, 'cp', split_axis=0, concat_axis=0, tiled=True)]
    ppermute x4 -> x0, starting transfers between devices: 5.33 us -> none  [shift(): return lax.ppermute(value, 'cp', [(i, (i + by) % n) for i in range(n)])]
    dot_general x1 -> x0, matrix products: 4.64 us -> none  [dot(): lax.dot_general(a, b, (((ca,), (cb,)), ((), ())), preferred_element_type=...]
  transfers between devices with their start and end apart: 8 -> 0, of which waited for: 5 -> 0; matrix products, arithmetic and copies ran while one was open for 7% -> 0% of each run, Pallas kernels for 0% -> 0%
where the time goes in v2:
time: 105 us
  Pallas kernels  98 us (93%)
  local copies, waits for them, and re-layouts  6.28 us (6%)
    pallas_call x1, Pallas kernels, on_device(): pl.pallas_call(functools.partial(kernel, ncp, ndp, side), out_shape=(jax....  98 us
    unnamed x13, local copies, waits for them, and re-layouts  6.28 us

profile of v2, /device:TPU:1, one launch (start us, length us, event | category | flops | bytes accessed | tf_op | source)
XLA Modules:
  0.0 104.9 jit_solution(13168439667260312086)
XLA Ops:
  0.6 98.0 %attention_backward.1 = (bf16[2,4096,128]{2,1,0:T(8,128)(2,1)}, bf16[2,128,2048]{2,1,0:T(8,128)(2,1)}, bf16[128,512]{1,0:T(8,128)(2,1)}, bf16[64,128]{1,0:T(8,128)(2,1)}, f32[56,576]{1,0:T(8,128)}) custom-call(s32[1,32]{1,0:T(1,128)} %lens.1, s32[1,8,8]{2,1,0:T(8,128)} %plan.1, bf16[2,4096,128]{2,1,0:T(8,128)(2,1)} %bitcast.14, ...), custom_call_target="tpu_custom_call" | custom-call | tf_op jit(solution)/shard_map/attention_backward/pallas_call | solution.py:422
  98.6 0.0 copy-start
  98.6 3.4 %copy.22 = bf16[2,1,128,32,128]{4,3,2,1,0:T(8,128)(2,1)} copy(bf16[2,1,128,32,128]{4,3,2,1,0:T(8,128)(2,1)} %bitcast.16) | data formatting | bytes 4194304
  102.0 0.0 copy-done
  102.0 0.0 copy-start.2
  102.0 0.0 copy-start.3
  102.0 0.0 copy-start.1
  102.0 1.0 copy.23
  103.0 0.0 copy-done.2
  103.0 0.7 copy.24
  103.6 0.0 copy-done.3
  103.6 0.6 copy.25
  104.2 0.0 copy-done.1
  104.2 0.7 copy.26
Async XLA Ops:
  98.6 3.4 %copy-start = (bf16[2,128,2048]{2,1,0:T(8,128)(2,1)S(1)}, bf16[2,128,2048]{2,1,0:T(8,128)(2,1)}, u32[]{:S(2)}) copy-start(bf16[2,128,2048]{2,1,0:T(8,128)(2,1)} %get-tuple-element.11) | copy-start | bytes 3145732
  102.0 1.0 copy-start.2
  102.0 1.7 %copy-start.3 = (bf16[64,128]{1,0:T(8,128)(2,1)S(1)}, bf16[64,128]{1,0:T(8,128)(2,1)}, u32[]{:S(2)}) copy-start(bf16[64,128]{1,0:T(8,128)(2,1)} %get-tuple-element.13) | copy-start | bytes 49156
  102.0 2.3 %copy-start.1 = (f32[56,576]{1,0:T(8,128)S(1)}, f32[56,576]{1,0:T(8,128)}, u32[]{:S(2)}) copy-start(f32[56,576]{1,0:T(8,128)} %get-tuple-element.29) | copy-start | bytes 387076

commit v3 on v2

v3 whole, which is shorter than its diff:
```python
import functools
import math

import jax
import jax.numpy as jnp
from jax import lax
from jax.experimental import pallas as pl
from jax.experimental.pallas import tpu as pltpu
from jax.sharding import PartitionSpec as P

BF = jnp.bfloat16
F32 = jnp.float32
MESH = pl.DeviceIdType.MESH
MARGIN = 192
SUB = 64
WIN = 256
HG = 8
ROPE = 64
COLUMNS = (slice(0, 384), slice(384, 640))
PIECE = 64


def dot(a, b, ca, cb):
    return lax.dot_general(a, b, (((ca,), (cb,)), ((), ())), preferred_element_type=F32)


def each(count, body):
    def step(i, carry):
        body(i)
        return carry

    lax.fori_loop(0, count, step, 0)


def kernel(
    ncp, ndp, side,
    lens, plan, qn_h, qr_h, go_h, lat_h, kr_h, hid_h, wk_h, wv_h,
    dqn_h, dqr_h, dlat, dkr, dw,
    qn, qr, go, le, kr, hid, wk, wv, qf, gf, of, ro, ql, gl, dq, kept, bias, acc, on, orp,
    slab, ht, hr, back, back1, back2, joined, jr, part, parts,
    sem_q, sem_w, sem_k, sem_halo, sem_hs, sem_hr, sem_os, sem_or, sem_oo, sem_back,
    sem_near, sem_fwd_s, sem_fwd_r, sem_ps, sem_pr, sem_own,
):
    layers, rows, head = qn.shape
    tok = qr.shape[1]
    heads = rows // tok
    lat = gl.shape[3]
    ext = le.shape[1]
    steps = heads // HG
    blk = tok // ncp
    part_heads = heads // 2
    part_wide = part_heads * ROPE
    scale = 1.0 / math.sqrt(head + ROPE)
    c_me = lax.axis_index("cp")
    d_me = lax.axis_index("dp")

    def cp_dev(offset):
        return lax.rem(c_me + offset + ncp, ncp)

    def dp_dev(offset):
        return lax.rem(d_me + offset + ndp, ndp)

    def q_copies(layer):
        return [
            pltpu.make_async_copy(qn_h.at[layer], qn.at[layer], sem_q.at[layer, 0]),
            pltpu.make_async_copy(go_h.at[layer], go.at[layer], sem_q.at[layer, 1]),
            pltpu.make_async_copy(qr_h.at[layer], qr.at[layer], sem_q.at[layer, 2]),
        ]

    def w_copies(layer, step):
        heads_of = pl.ds(step * HG, HG)
        return [
            pltpu.make_async_copy(wk_h.at[layer, heads_of], wk.at[layer, heads_of], sem_w.at[layer, step, 0]),
            pltpu.make_async_copy(wv_h.at[layer, heads_of], wv.at[layer, heads_of], sem_w.at[layer, step, 1]),
        ]

    own_rows = slice(MARGIN, MARGIN + tok)
    edge = MARGIN - tok
    k_copies = [
        pltpu.make_async_copy(lat_h, le.at[own_rows, :lat], sem_k.at[0]),
        pltpu.make_async_copy(kr_h, kr, sem_k.at[1]),
        pltpu.make_async_copy(hid_h, hid, sem_k.at[2]),
    ]
    for c in k_copies:
        c.start()
    for layer in range(layers):
        for c in q_copies(layer):
            c.start()
        for step in range(steps):
            for c in w_copies(layer, step):
                c.start()

    barrier = pltpu.get_barrier_semaphore()

    def greet_cp(i):
        pl.semaphore_signal(barrier, inc=1, device_id=(cp_dev(i + 1), d_me), device_id_type=MESH)

    def greet_dp(i):
        pl.semaphore_signal(barrier, inc=1, device_id=(c_me, dp_dev(i + 1)), device_id_type=MESH)

    each(ncp - 1, greet_cp)
    each(ndp - 1, greet_dp)

    k_copies[0].wait()
    k_copies[1].wait()
    turned = kr[...].astype(F32)
    le[own_rows, lat:] = jnp.concatenate([turned, turned], axis=0).T.astype(BF)
    pl.semaphore_wait(barrier, ncp + ndp - 2)

    halo = [
        pltpu.make_async_remote_copy(
            le.at[own_rows], le.at[edge:MARGIN], sem_halo.at[0], sem_halo.at[1],
            device_id=(cp_dev(1), d_me), device_id_type=MESH,
        ),
        pltpu.make_async_remote_copy(
            le.at[MARGIN + tok - edge : MARGIN + tok], le.at[:edge], sem_halo.at[2], sem_halo.at[3],
            device_id=(cp_dev(2), d_me), device_id_type=MESH,
        ),
    ]
    for c in halo:
        c.start()

    k_copies[2].wait()
    width = hid.shape[1] // ncp
    rows_dev = width // ndp

    def turn(c):
        for j in range(width // 128):
            lanes = pl.ds(pl.multiple_of(c * width + j * 128, 128), 128)
            slab[j * 128 : j * 128 + 128, :] = hid[:, lanes].astype(F32).T
        pad = jnp.zeros((PIECE - rows_dev, tok), F32)
        for j in range(ndp):
            piece = jnp.concatenate([slab[j * rows_dev : (j + 1) * rows_dev, :], pad], axis=0)
            ht[j, pl.ds(pl.multiple_of(c * PIECE, PIECE), PIECE), :] = piece.astype(BF)

    each(ncp, turn)

    def my_lanes():
        return pl.ds(pl.multiple_of(d_me * tok, tok), tok)

    def hidden_copy(i):
        to = dp_dev(i + 1)
        return pltpu.make_async_remote_copy(
            ht.at[to], hr.at[:, my_lanes()], sem_hs.at[i], sem_hr.at[i],
            device_id=(c_me, to), device_id_type=MESH,
        )

    each(ndp - 1, lambda i: hidden_copy(i).start())
    hidden_own = pltpu.make_async_copy(ht.at[d_me], hr.at[:, my_lanes()], sem_own.at[0])
    hidden_own.start()

    acc[...] = jnp.zeros_like(acc)
    for s in range(2):
        t = c_me * tok + s * SUB + lax.broadcasted_iota(jnp.int32, (SUB, 128), 0)
        first = jnp.zeros((SUB, 128), jnp.int32)
        end = jnp.int32(0)
        for j in range(lens.shape[1]):
            end = end + lens[0, j]
            first = jnp.where(end <= t, end, first)
        for half in range(2):
            u = (
                c_me * tok - MARGIN + s * SUB + half * 128
                + lax.broadcasted_iota(jnp.int32, (SUB, 128), 1)
            )
            ok = (u >= first) & (u <= t)
            bias[s, :, half * 128 : half * 128 + 128] = jnp.where(ok, jnp.inf, -jnp.inf)
    low = lax.broadcasted_iota(jnp.int32, (SUB, 128), 1) < ROPE

    def out_parts(layer, half, to):
        tokens = pl.ds(pl.multiple_of(c_me * blk, blk), blk)
        return [
            (on.at[to, layer, half], dqn_h.at[layer, tokens, pl.ds(half * part_heads, part_heads)]),
            (orp.at[to, layer, half], dqr_h.at[layer, tokens, pl.ds(half * part_wide, part_wide)]),
        ]

    def out_copies(layer, half, i):
        to = cp_dev(i + 1)
        return [
            pltpu.make_async_remote_copy(
                src, dst, sem_os.at[layer, half, i, j], sem_or.at[layer, half, i, j],
                device_id=(to, d_me), device_id_type=MESH,
            )
            for j, (src, dst) in enumerate(out_parts(layer, half, to))
        ]

    def out_own(layer, half):
        return [
            pltpu.make_async_copy(src, dst, sem_oo.at[layer, half, j])
            for j, (src, dst) in enumerate(out_parts(layer, half, c_me))
        ]

    def widen(layer):
        for c in q_copies(layer):
            c.wait()

        def chunk(c):
            piece = pl.ds(pl.multiple_of(c * 512, 512), 512)
            qf[layer, piece, :] = qn[layer, piece, :].astype(F32)
            gf[layer, piece, :] = go[layer, piece, :].astype(F32)

        each(rows // 512, chunk)

    def absorb(n, slot, i):
        layer, step = n // steps, lax.rem(n, steps)
        h = step * HG + i
        a = dot(qf[layer, pl.ds(h, tok, stride=heads), :].astype(BF), wk[layer, h], 1, 0).astype(BF)
        b = dot(gf[layer, pl.ds(h, tok, stride=heads), :].astype(BF), wv[layer, h], 1, 1).astype(BF)
        lanes = pl.ds(pl.multiple_of((step * (HG // 2) + i // 2) * 128, 128), 128)
        mine = slice(i * SUB, i * SUB + SUB)
        for s in range(2):
            sub = slice(s * SUB, s * SUB + SUB)
            ql[slot, s, mine, :lat] = a[sub]
            gl[slot, s, mine, :] = b[sub]
            pair = qr[layer, sub, lanes].astype(F32)
            pair = jnp.where(low if i % 2 == 0 else ~low, pair, 0.0)
            ql[slot, s, mine, lat:] = pair.astype(BF)

    def scores(slot, s):
        win = slice(s * SUB, s * SUB + WIN)
        return dot(ql[slot, s], le[win, :], 1, 1), dot(gl[slot, s], le[win, :lat], 1, 1)

    def softmax(s, score, dprob, j):
        part_of = slice(j * 2 * SUB, (j + 1) * 2 * SUB)
        x = jnp.minimum(score[part_of].reshape(2, SUB, WIN), bias[s][None]).reshape(2 * SUB, WIN)
        e = jnp.exp((x - jnp.max(x, axis=1, keepdims=True)) * scale)
        d = dprob[part_of]
        inv = 1.0 / jnp.sum(e, axis=1, keepdims=True)
        delta = jnp.sum(e * d, axis=1, keepdims=True) * inv
        return (e * (inv * scale) * (d - delta)).astype(BF), (e * inv).astype(BF)

    def add_keys(slot, s, ds, low_p):
        win = slice(s * SUB, s * SUB + WIN)
        acc[win, :] += dot(ds, ql[slot, s], 0, 0)
        acc[win, :lat] += dot(low_p, gl[slot, s], 0, 0)

    def query_side(step, s, ds):
        win = slice(s * SUB, s * SUB + WIN)
        d = dot(ds, le[win, :], 1, 0)
        for i in range(HG):
            dq[i, s * SUB : s * SUB + SUB, :] = d[i * SUB : i * SUB + SUB, :lat].astype(BF)
        for j in range(HG // 2):
            even = d[2 * j * SUB : (2 * j + 1) * SUB, lat:]
            odd = d[(2 * j + 1) * SUB : (2 * j + 2) * SUB, lat:]
            both = jnp.where(low, even, odd).astype(BF)
            lanes = pl.ds(pl.multiple_of((lax.rem(step, 2) * (HG // 2) + j) * 128, 128), 128)
            for q in range(SUB // blk):
                ro[s * (SUB // blk) + q, :, lanes] = both[q * blk : q * blk + blk]

    def query_out(layer, step):
        for i in range(HG):
            back_q = dot(dq[i], wk[layer, step * HG + i], 1, 1)
            for q in range(ncp):
                of[q, pl.ds(lax.rem(step, 2) * HG + i, blk, stride=part_heads), :] = back_q[q * blk : q * blk + blk]

    def send_out(layer, half):
        def place(k):
            b = plan[0, c_me, k]
            on[k, layer, half] = of[b].astype(BF).reshape(blk, part_heads, head)
            orp[k, layer, half] = ro[b]

        each(ncp, place)

        def start(i):
            for c in out_copies(layer, half, i):
                c.start()

        each(ncp - 1, start)
        for c in out_own(layer, half):
            c.start()

    def step_body(n, layer, defer):
        slot = lax.rem(n, 2)
        follow = jnp.minimum(n + 1, layers * steps - 1)

        @pl.when(n + 1 < layers * steps)
        def _():
            for c in w_copies(follow // steps, lax.rem(follow, steps)):
                c.wait()

        step = n - layer * steps
        pend = None
        for s in range(2):
            score, dprob = scores(slot, s)
            if pend is not None:
                add_keys(slot, *pend)
                if not defer:
                    query_side(step, pend[0], pend[1])
            ds, low_p = [], []
            for j in range(HG // 2):
                x, p = softmax(s, score, dprob, j)
                ds.append(x)
                low_p.append(p)
                absorb(follow, 1 - slot, s * (HG // 2) + j)
            ds = jnp.concatenate(ds, axis=0)
            low_p = jnp.concatenate(low_p, axis=0)
            if defer:
                kept[step, s] = ds
            pend = (s, ds, low_p)
        add_keys(slot, *pend)
        if not defer:
            query_side(step, pend[0], pend[1])
            query_out(layer, step)

            @pl.when(lax.rem(step, 2) == 1)
            def _():
                send_out(layer, step // 2)

    back_copies = [
        pltpu.make_async_remote_copy(
            back.at[edge:MARGIN], back1, sem_back.at[0], sem_back.at[1],
            device_id=(cp_dev(-1), d_me), device_id_type=MESH,
        ),
        pltpu.make_async_remote_copy(
            back.at[:edge], back2, sem_back.at[2], sem_back.at[3],
            device_id=(cp_dev(-2), d_me), device_id_type=MESH,
        ),
    ]

    for layer in range(layers):
        widen(layer)
    for c in w_copies(0, 0):
        c.wait()
    for i in range(HG):
        absorb(jnp.int32(0), 0, i)
    for c in halo:
        c.wait_recv()

    last = layers - 1
    each(last * steps, lambda n: step_body(n, n // steps, False))
    each(steps, lambda n: step_body(n + last * steps, last, True))
    back[...] = acc[:MARGIN, :].astype(BF)
    for c in back_copies:
        c.start()

    def late_queries(step):
        for s in range(2):
            query_side(step, s, kept[step, s])
        query_out(last, step)

    each(2, late_queries)
    send_out(last, 0)

    for c in back_copies:
        c.wait_recv()
    total = acc[own_rows, :] + back1[...].astype(F32)
    late = total[tok - edge :] + back2[...].astype(F32)
    total = jnp.concatenate([total[: tok - edge], late], axis=0)
    rope = total[:, lat:]
    rope = rope + pltpu.roll(rope, ROPE, 1)
    low_all = lax.broadcasted_iota(jnp.int32, (tok, 128), 1) < ROPE
    rope = jnp.where(low_all, rope, 0.0)
    joined[:, :lat] = total[:, :lat].astype(BF)
    joined[:, lat:] = rope.astype(BF)
    dlat[...] = total[:, :lat].astype(BF)
    dkr[...] = rope.T[:ROPE].astype(BF)

    y, z = d_me // side, lax.rem(d_me, side)
    other = ndp // side
    half = tok // 2

    def place_of(yy, zz, which, ch):
        rows_of = pl.ds(pl.multiple_of((yy * side + zz) * tok + which * half, half), half)
        return jr.at[rows_of, COLUMNS[ch]]

    def ring(value, offset, n):
        return lax.rem(value + offset + n, n)

    def near(ch, which, k):
        lanes = COLUMNS[ch]
        src = joined.at[which * half : which * half + half, lanes]
        to = y * side + ring(z, k, side) if which == 0 else ring(y, k, other) * side + z
        return pltpu.make_async_remote_copy(
            src, place_of(y, z, which, ch), sem_near.at[ch, which, 0, k - 1], sem_near.at[ch, which, 1, k - 1],
            device_id=(c_me, to), device_id_type=MESH,
        )

    def forward(ch, which, j, k):
        if which == 0:
            ref = place_of(y, ring(z, -j, side), 0, ch)
            to = ring(y, k, other) * side + z
        else:
            ref = place_of(ring(y, -j, other), z, 1, ch)
            to = y * side + ring(z, k, side)
        src = joined.at[which * half : which * half + half, COLUMNS[ch]] if j == 0 else ref
        return pltpu.make_async_remote_copy(
            src, ref, sem_fwd_s.at[ch, which, j, k - 1], sem_fwd_r.at[ch, which, j, k - 1],
            device_id=(c_me, to), device_id_type=MESH,
        )

    for ch in range(len(COLUMNS)):
        for k in (1, 3, 2):
            near(ch, 0, k).start()
            near(ch, 1, k).start()
        for k in (1, 3, 2):
            forward(ch, 0, 0, k).start()
            forward(ch, 1, 0, k).start()
    gather_own = pltpu.make_async_copy(
        joined, jr.at[pl.ds(pl.multiple_of(d_me * tok, tok), tok)], sem_own.at[0]
    )
    hidden_own.wait()
    gather_own.start()
    each(2, lambda i: late_queries(i + 2))
    send_out(last, 1)
    for ch in range(len(COLUMNS)):
        for j in (1, 3, 2):
            for which in range(2):
                near(ch, which, j).wait_recv()
                for k in (1, 3, 2):
                    forward(ch, which, j, k).start()
    each(ndp - 1, lambda i: hidden_copy(i).wait())
    gather_own.wait()

    def part_copy(ch, i):
        to = cp_dev(i + 1)
        return pltpu.make_async_remote_copy(
            part.at[pl.ds(pl.multiple_of(to * PIECE, PIECE), PIECE), COLUMNS[ch]],
            parts.at[i, :, COLUMNS[ch]],
            sem_ps.at[ch, i], sem_pr.at[ch, i], device_id=(to, d_me), device_id_type=MESH,
        )

    for ch in range(len(COLUMNS)):
        for j in range(4):
            for which in range(2):
                for k in (1, 2, 3):
                    forward(ch, which, j, k).wait_recv()

        def product(c):
            piece = pl.ds(pl.multiple_of(c * 256, 256), 256)
            part[piece, COLUMNS[ch]] = dot(hr[piece, :], jr[:, COLUMNS[ch]], 1, 0).astype(BF)

        each(part.shape[0] // 256, product)
        each(ncp - 1, lambda i: part_copy(ch, i).start())
    for ch in range(len(COLUMNS)):
        cols = COLUMNS[ch]
        mine = part[pl.ds(pl.multiple_of(c_me * PIECE, PIECE), PIECE), cols].astype(F32)
        for i in range(ncp - 1):
            part_copy(ch, i).wait_recv()
            mine = mine + parts[i, :, cols].astype(F32)
        width_now = min(cols.stop, lat + ROPE) - cols.start
        dw[:, cols.start : cols.start + width_now] = mine[:rows_dev, :width_now]

    for c in halo + back_copies:
        c.wait_send()
    for ch in range(len(COLUMNS)):
        for which in range(2):
            for k in (1, 2, 3):
                near(ch, which, k).wait_send()
            for j in range(4):
                for k in (1, 2, 3):
                    forward(ch, which, j, k).wait_send()
        each(ncp - 1, lambda i: part_copy(ch, i).wait_send())

    def finish(n):
        layer, half = n // 2, lax.rem(n, 2)
        for c in out_own(layer, half):
            c.wait()

        def one(i):
            for c in out_copies(layer, half, i):
                c.wait()

        each(ncp - 1, one)

    each(2 * layers, finish)


def pass_on(*refs):
    count = (len(refs) - 2) // 3
    came, went = refs[-2:]
    moves = []
    for i in range(count):
        src, dst, held = refs[i], refs[count + i], refs[2 * count + i]
        pieces = [(0, slice(None))]
        if len(src.shape) > 2:
            cut = src.shape[1] // 4
            pieces = [(n, (n // 4, slice(n % 4 * cut, (n % 4 + 1) * cut))) for n in range(4 * src.shape[0])]
        for n, at in pieces:
            moves.append(
                (
                    pltpu.make_async_copy(src.at[at], held.at[at], came.at[i, n]),
                    pltpu.make_async_copy(held.at[at], dst.at[at], went.at[i, n]),
                )
            )
    for load, _ in moves:
        load.start()
    for load, store in moves:
        load.wait()
        store.start()
    for _, store in moves:
        store.wait()


def on_device(q_nope, q_rope, grad_out, latent, key_rope, hidden_in, w_uk, w_uv, doc_lengths, plan):
    ncp = lax.axis_size("cp")
    ndp = lax.axis_size("dp")
    side = math.isqrt(ndp)
    layers, _, tok, heads, head = q_nope.shape
    wide = q_rope.shape[3]
    lat = latent.shape[2]
    model = hidden_in.shape[2]
    ext = lat + 2 * ROPE
    rows = tok * heads
    smem = pl.BlockSpec(memory_space=pltpu.SMEM)
    hbm = pl.BlockSpec(memory_space=pl.ANY)
    vmem = pl.BlockSpec(memory_space=pltpu.VMEM)
    dma = pltpu.SemaphoreType.DMA
    results = pl.pallas_call(
        functools.partial(kernel, ncp, ndp, side),
        out_shape=(
            jax.ShapeDtypeStruct((layers, tok, heads, head), BF),
            jax.ShapeDtypeStruct((layers, tok, wide), BF),
            jax.ShapeDtypeStruct((tok, lat), BF),
            jax.ShapeDtypeStruct((ROPE, tok), BF),
            jax.ShapeDtypeStruct((model // (ncp * ndp), lat + ROPE), F32),
        ),
        in_specs=[smem, smem] + [hbm] * 8,
        out_specs=(hbm, hbm, vmem, vmem, vmem),
        scratch_shapes=[
            pltpu.VMEM((layers, rows, head), BF),
            pltpu.VMEM((layers, tok, wide), BF),
            pltpu.VMEM((layers, rows, head), BF),
            pltpu.VMEM((MARGIN + tok, ext), BF),
            pltpu.VMEM((ROPE, tok), BF),
            pltpu.VMEM((tok, model), BF),
            pltpu.VMEM(w_uk.shape, BF),
            pltpu.VMEM(w_uv.shape, BF),
            pltpu.VMEM((layers, rows, head), F32),
            pltpu.VMEM((layers, rows, head), F32),
            pltpu.VMEM((ncp, rows // ncp // 2, head), F32),
            pltpu.VMEM((ncp, tok // ncp, wide // 2), BF),
            pltpu.VMEM((2, 2, HG * SUB, ext), BF),
            pltpu.VMEM((2, 2, HG * SUB, lat), BF),
            pltpu.VMEM((HG, tok, lat), BF),
            pltpu.VMEM((heads // HG, 2, HG * SUB, WIN), BF),
            pltpu.VMEM((2, SUB, WIN), F32),
            pltpu.VMEM((MARGIN + tok, ext), F32),
            pltpu.VMEM((ncp, layers, 2, tok // ncp, heads // 2, head), BF),
            pltpu.VMEM((ncp, layers, 2, tok // ncp, wide // 2), BF),
            pltpu.VMEM((model // ncp, tok), F32),
            pltpu.VMEM((ndp, ncp * PIECE, tok), BF),
            pltpu.VMEM((ncp * PIECE, ndp * tok), BF),
            pltpu.VMEM((MARGIN, ext), BF),
            pltpu.VMEM((tok, ext), BF),
            pltpu.VMEM((MARGIN - tok, ext), BF),
            pltpu.VMEM((tok, ext), BF),
            pltpu.VMEM((ndp * tok, ext), BF),
            pltpu.VMEM((ncp * PIECE, ext), BF),
            pltpu.VMEM((ncp - 1, PIECE, ext), BF),
            dma((layers, 3)),
            dma((layers, heads // HG, 2)),
            dma((3,)),
            dma((4,)),
            dma((ndp - 1,)),
            dma((ndp - 1,)),
            dma((layers, 2, ncp - 1, 2)),
            dma((layers, 2, ncp - 1, 2)),
            dma((layers, 2, 2)),
            dma((4,)),
            dma((len(COLUMNS), 2, 2, 3)),
            dma((len(COLUMNS), 2, 4, 3)),
            dma((len(COLUMNS), 2, 4, 3)),
            dma((len(COLUMNS), ncp - 1)),
            dma((len(COLUMNS), ncp - 1)),
            dma((1,)),
        ],
        compiler_params=pltpu.CompilerParams(
            collective_id=0, has_side_effects=True, vmem_limit_bytes=60 * 1024 * 1024
        ),
        name="attention_backward",
    )(
        doc_lengths,
        plan,
        q_nope.reshape(layers, rows, head),
        q_rope[:, 0],
        grad_out.reshape(layers, rows, head),
        latent[0],
        key_rope[0],
        hidden_in[0],
        w_uk,
        w_uv,
    )
    dqn, dqr, dlat, dkr, dw = pl.pallas_call(
        pass_on,
        out_shape=tuple(jax.ShapeDtypeStruct(r.shape, r.dtype) for r in results),
        in_specs=[hbm] * 5,
        out_specs=(hbm,) * 5,
        scratch_shapes=[pltpu.VMEM(r.shape, r.dtype) for r in results] + [dma((5, 8)), dma((5, 8))],
        name="pass_on",
    )(*results)
    return (
        dqn.reshape(q_nope.shape),
        dqr.reshape(q_rope.shape),
        dlat[None],
        dkr[None],
        dw,
    )


def solution(mesh):
    placed = (
        P(None, "dp", "cp", None, None),
        P(None, "dp", "cp", None),
        P(None, "dp", "cp", None, None),
        P("dp", "cp", None),
        P("dp", None, "cp"),
        P("dp", "cp", None),
        P(),
        P(),
        P("dp", None),
        P("dp", None, None),
    )
    return jax.shard_map(
        on_device,
        mesh=mesh,
        in_specs=placed,
        out_specs=(
            P(None, "dp", "cp", None, None),
            P(None, "dp", "cp", None),
            P("dp", "cp", None),
            P("dp", None, "cp"),
            P(("cp", "dp"), None),
        ),
        check_vma=False,
    )
```

time: 105 us -> 88.3 us (0.84)
  Pallas kernels: 98 us -> 87.5 us
  local copies, waits for them, and re-layouts: 6.28 us -> 0 us
    pallas_call x1, Pallas kernels: 98 us -> 84.1 us  [on_device(): pl.pallas_call(functools.partial(kernel, ncp, ndp, side), out_shape=(jax....]
    unnamed x13 -> x0, local copies, waits for them, and re-layouts: 6.28 us -> none
    pallas_call x0 -> x1, Pallas kernels: none -> 3.41 us  [on_device(): pl.pallas_call(pass_on, out_shape=tuple((jax.ShapeDtypeStruct(r.shape, r....]
where the time goes in v3:
time: 88.3 us; the launch traced here: 88.2 us
  Pallas kernels  87.5 us (99%)
    pallas_call x1, Pallas kernels, on_device(): pl.pallas_call(functools.partial(kernel, ncp, ndp, side), out_shape=(jax....  84.1 us
    pallas_call x1, Pallas kernels, on_device(): pl.pallas_call(pass_on, out_shape=tuple((jax.ShapeDtypeStruct(r.shape, r....  3.41 us

profile of v3, /device:TPU:1, one launch (start us, length us, event | category | flops | bytes accessed | tf_op | source)
XLA Modules:
  0.0 88.2 jit_solution(14998471479938964260)
XLA Ops:
  0.6 84.1 %attention_backward.1 = (bf16[2,128,32,128]{3,2,1,0:T(8,128)(2,1)}, bf16[2,128,2048]{2,1,0:T(8,128)(2,1)}, bf16[128,512]{1,0:T(8,128)(2,1)}, bf16[64,128]{1,0:T(8,128)(2,1)}, f32[56,576]{1,0:T(8,128)}) custom-call(s32[1,32]{1,0:T(1,128)} %lens.1, s32[1,8,8]{2,1,0:T(8,128)} %plan.1, bf16[2,4096,128]{2,1,0:T(8,128)(2,1)} %bitcast.14, ...), custom_call_target="tpu_custom_call" | custom-call | tf_op jit(solution)/shard_map/attention_backward/pallas_call | solution.py:507
  84.8 3.4 %pass_on.1 = (bf16[2,128,32,128]{3,2,1,0:T(8,128)(2,1)}, bf16[2,128,2048]{2,1,0:T(8,128)(2,1)}, bf16[128,512]{1,0:T(8,128)(2,1)}, bf16[64,128]{1,0:T(8,128)(2,1)}, f32[56,576]{1,0:T(8,128)}) custom-call(bf16[2,128,32,128]{3,2,1,0:T(8,128)(2,1)} %get-tuple-element.15.refs_0_, bf16[2,128,2048]{2,1,0:T(8,128)(2,1)} %get-tuple-element.16.refs_1_, ...), custom_call_target="tpu_custom_call" | custom-call | tf_op jit(solution)/shard_map/pass_on/pallas_call | solution.py:582

commit v4 on v3

--- a/solution.py
+++ b/solution.py
@@ -15,8 +15,10 @@
 SUB = 64
 WIN = 256
 HG = 8
+PITCH = 36
+OUT_PITCH = 20
 ROPE = 64
-COLUMNS = (slice(0, 384), slice(384, 640))
+FIRST = 384
 PIECE = 64
 
 
@@ -37,9 +39,9 @@
     lens, plan, qn_h, qr_h, go_h, lat_h, kr_h, hid_h, wk_h, wv_h,
     dqn_h, dqr_h, dlat, dkr, dw,
     qn, qr, go, le, kr, hid, wk, wv, qf, gf, of, ro, ql, gl, dq, kept, bias, acc, on, orp,
-    slab, ht, hr, back, back1, back2, joined, jr, part, parts,
+    slab, ht, hr, back, back1, back2, ja, jb, ga, gb, gc, pa, pb, ra, rb,
     sem_q, sem_w, sem_k, sem_halo, sem_hs, sem_hr, sem_os, sem_or, sem_oo, sem_back,
-    sem_near, sem_fwd_s, sem_fwd_r, sem_ps, sem_pr, sem_own,
+    sem_near, sem_fwd_s, sem_fwd_r, sem_rel, sem_ps, sem_pr, sem_own,
 ):
     layers, rows, head = qn.shape
     tok = qr.shape[1]
@@ -81,14 +83,8 @@
         pltpu.make_async_copy(kr_h, kr, sem_k.at[1]),
         pltpu.make_async_copy(hid_h, hid, sem_k.at[2]),
     ]
-    for c in k_copies:
+    for c in k_copies[:2] + q_copies(0) + w_copies(0, 0):
         c.start()
-    for layer in range(layers):
-        for c in q_copies(layer):
-            c.start()
-        for step in range(steps):
-            for c in w_copies(layer, step):
-                c.start()
 
     barrier = pltpu.get_barrier_semaphore()
 
@@ -119,35 +115,6 @@
     ]
     for c in halo:
         c.start()
-
-    k_copies[2].wait()
-    width = hid.shape[1] // ncp
-    rows_dev = width // ndp
-
-    def turn(c):
-        for j in range(width // 128):
-            lanes = pl.ds(pl.multiple_of(c * width + j * 128, 128), 128)
-            slab[j * 128 : j * 128 + 128, :] = hid[:, lanes].astype(F32).T
-        pad = jnp.zeros((PIECE - rows_dev, tok), F32)
-        for j in range(ndp):
-            piece = jnp.concatenate([slab[j * rows_dev : (j + 1) * rows_dev, :], pad], axis=0)
-            ht[j, pl.ds(pl.multiple_of(c * PIECE, PIECE), PIECE), :] = piece.astype(BF)
-
-    each(ncp, turn)
-
-    def my_lanes():
-        return pl.ds(pl.multiple_of(d_me * tok, tok), tok)
-
-    def hidden_copy(i):
-        to = dp_dev(i + 1)
-        return pltpu.make_async_remote_copy(
-            ht.at[to], hr.at[:, my_lanes()], sem_hs.at[i], sem_hr.at[i],
-            device_id=(c_me, to), device_id_type=MESH,
-        )
-
-    each(ndp - 1, lambda i: hidden_copy(i).start())
-    hidden_own = pltpu.make_async_copy(ht.at[d_me], hr.at[:, my_lanes()], sem_own.at[0])
-    hidden_own.start()
 
     acc[...] = jnp.zeros_like(acc)
     for s in range(2):
@@ -194,17 +161,20 @@
             c.wait()
 
         def chunk(c):
-            piece = pl.ds(pl.multiple_of(c * 512, 512), 512)
-            qf[layer, piece, :] = qn[layer, piece, :].astype(F32)
-            gf[layer, piece, :] = go[layer, piece, :].astype(F32)
-
-        each(rows // 512, chunk)
+            piece = pl.ds(pl.multiple_of(c * blk * heads, blk * heads), blk * heads)
+            for wide_ref, ref in ((qf, qn), (gf, go)):
+                value = ref[layer, piece, :].astype(F32)
+                for t in range(blk):
+                    at = pl.ds(c * (blk * PITCH) + t * PITCH, heads)
+                    wide_ref[layer, at, :] = value[t * heads : (t + 1) * heads]
+
+        each(tok // blk, chunk)
 
     def absorb(n, slot, i):
         layer, step = n // steps, lax.rem(n, steps)
         h = step * HG + i
-        a = dot(qf[layer, pl.ds(h, tok, stride=heads), :].astype(BF), wk[layer, h], 1, 0).astype(BF)
-        b = dot(gf[layer, pl.ds(h, tok, stride=heads), :].astype(BF), wv[layer, h], 1, 1).astype(BF)
+        a = dot(qf[layer, pl.ds(h, tok, stride=PITCH), :].astype(BF), wk[layer, h], 1, 0).astype(BF)
+        b = dot(gf[layer, pl.ds(h, tok, stride=PITCH), :].astype(BF), wv[layer, h], 1, 1).astype(BF)
         lanes = pl.ds(pl.multiple_of((step * (HG // 2) + i // 2) * 128, 128), 128)
         mine = slice(i * SUB, i * SUB + SUB)
         for s in range(2):
@@ -250,12 +220,13 @@
         for i in range(HG):
             back_q = dot(dq[i], wk[layer, step * HG + i], 1, 1)
             for q in range(ncp):
-                of[q, pl.ds(lax.rem(step, 2) * HG + i, blk, stride=part_heads), :] = back_q[q * blk : q * blk + blk]
+                of[q, pl.ds(lax.rem(step, 2) * HG + i, blk, stride=OUT_PITCH), :] = back_q[q * blk : q * blk + blk]
 
     def send_out(layer, half):
         def place(k):
             b = plan[0, c_me, k]
-            on[k, layer, half] = of[b].astype(BF).reshape(blk, part_heads, head)
+            for t in range(blk):
+                on[k, layer, half, t] = of[b, t * OUT_PITCH : t * OUT_PITCH + part_heads, :].astype(BF)
             orp[k, layer, half] = ro[b]
 
         each(ncp, place)
@@ -268,16 +239,27 @@
         for c in out_own(layer, half):
             c.start()
 
-    def step_body(n, layer, defer):
+    def step_body(n, layer, defer, more):
         slot = lax.rem(n, 2)
-        follow = jnp.minimum(n + 1, layers * steps - 1)
-
-        @pl.when(n + 1 < layers * steps)
-        def _():
+        follow = n + 1
+        step = n - layer * steps
+        if not defer:
+
+            @pl.when(step == 1)
+            def _():
+                widen(layer + 1)
+
+        if more:
+            ahead = n + 3
+
+            @pl.when(ahead < layers * steps)
+            def _():
+                for c in w_copies(ahead // steps, lax.rem(ahead, steps)):
+                    c.start()
+
             for c in w_copies(follow // steps, lax.rem(follow, steps)):
                 c.wait()
 
-        step = n - layer * steps
         pend = None
         for s in range(2):
             score, dprob = scores(slot, s)
@@ -290,7 +272,8 @@
                 x, p = softmax(s, score, dprob, j)
                 ds.append(x)
                 low_p.append(p)
-                absorb(follow, 1 - slot, s * (HG // 2) + j)
+                if more:
+                    absorb(follow, 1 - slot, s * (HG // 2) + j)
             ds = jnp.concatenate(ds, axis=0)
             low_p = jnp.concatenate(low_p, axis=0)
             if defer:
@@ -316,18 +299,52 @@
         ),
     ]
 
-    for layer in range(layers):
-        widen(layer)
+    widen(0)
+    for c in k_copies[2:] + w_copies(0, 1):
+        c.start()
     for c in w_copies(0, 0):
         c.wait()
+    for c in q_copies(1) + w_copies(0, 2):
+        c.start()
     for i in range(HG):
         absorb(jnp.int32(0), 0, i)
+
+    k_copies[2].wait()
+    width = hid.shape[1] // ncp
+    rows_dev = width // ndp
+
+    def turn(c):
+        for j in range(width // 128):
+            lanes = pl.ds(pl.multiple_of(c * width + j * 128, 128), 128)
+            slab[j * 128 : j * 128 + 128, :] = hid[:, lanes].astype(F32).T
+        pad = jnp.zeros((PIECE - rows_dev, tok), F32)
+        for j in range(ndp):
+            piece = jnp.concatenate([slab[j * rows_dev : (j + 1) * rows_dev, :], pad], axis=0)
+            ht[j, pl.ds(pl.multiple_of(c * PIECE, PIECE), PIECE), :] = piece.astype(BF)
+
+    each(ncp, turn)
+
+    def my_lanes():
+        return pl.ds(pl.multiple_of(d_me * tok, tok), tok)
+
+    def hidden_copy(i):
+        to = dp_dev(i + 1)
+        return pltpu.make_async_remote_copy(
+            ht.at[to], hr.at[:, my_lanes()], sem_hs.at[i], sem_hr.at[i],
+            device_id=(c_me, to), device_id_type=MESH,
+        )
+
+    each(ndp - 1, lambda i: hidden_copy(i).start())
+    hidden_own = pltpu.make_async_copy(ht.at[d_me], hr.at[:, my_lanes()], sem_own.at[0])
+    hidden_own.start()
+
     for c in halo:
         c.wait_recv()
 
     last = layers - 1
-    each(last * steps, lambda n: step_body(n, n // steps, False))
-    each(steps, lambda n: step_body(n + last * steps, last, True))
+    each(last * steps, lambda n: step_body(n, n // steps, False, True))
+    each(steps - 1, lambda n: step_body(n + last * steps, last, True, True))
+    step_body(jnp.int32(layers * steps - 1), last, True, False)
     back[...] = acc[:MARGIN, :].astype(BF)
     for c in back_copies:
         c.start()
@@ -349,25 +366,34 @@
     rope = rope + pltpu.roll(rope, ROPE, 1)
     low_all = lax.broadcasted_iota(jnp.int32, (tok, 128), 1) < ROPE
     rope = jnp.where(low_all, rope, 0.0)
-    joined[:, :lat] = total[:, :lat].astype(BF)
-    joined[:, lat:] = rope.astype(BF)
+    half = tok // 2
+    quarter = half // 2
+    for w in range(2):
+        of_half = slice(w * half, w * half + half)
+        ja[of_half, :] = total[of_half, :FIRST].astype(BF)
+        jb[w, :half, :] = total[of_half, FIRST:lat].astype(BF)
+        top = rope[w * half : w * half + quarter]
+        bottom = pltpu.roll(rope[w * half + quarter : (w + 1) * half], ROPE, 1)
+        jb[w, half:, :] = (top + bottom).astype(BF)
     dlat[...] = total[:, :lat].astype(BF)
     dkr[...] = rope.T[:ROPE].astype(BF)
 
     y, z = d_me // side, lax.rem(d_me, side)
     other = ndp // side
-    half = tok // 2
 
     def place_of(yy, zz, which, ch):
-        rows_of = pl.ds(pl.multiple_of((yy * side + zz) * tok + which * half, half), half)
-        return jr.at[rows_of, COLUMNS[ch]]
+        if ch == 1:
+            return gb.at[yy * side + zz, which]
+        return ga.at[pl.ds(pl.multiple_of((yy * side + zz) * tok + which * half, half), half)]
+
+    def mine_of(which, ch):
+        return jb.at[which] if ch == 1 else ja.at[which * half : which * half + half]
 
     def ring(value, offset, n):
         return lax.rem(value + offset + n, n)
 
     def near(ch, which, k):
-        lanes = COLUMNS[ch]
-        src = joined.at[which * half : which * half + half, lanes]
+        src = mine_of(which, ch)
         to = y * side + ring(z, k, side) if which == 0 else ring(y, k, other) * side + z
         return pltpu.make_async_remote_copy(
             src, place_of(y, z, which, ch), sem_near.at[ch, which, 0, k - 1], sem_near.at[ch, which, 1, k - 1],
@@ -381,73 +407,133 @@
         else:
             ref = place_of(ring(y, -j, other), z, 1, ch)
             to = y * side + ring(z, k, side)
-        src = joined.at[which * half : which * half + half, COLUMNS[ch]] if j == 0 else ref
+        src = mine_of(which, ch) if j == 0 else ref
         return pltpu.make_async_remote_copy(
             src, ref, sem_fwd_s.at[ch, which, j, k - 1], sem_fwd_r.at[ch, which, j, k - 1],
             device_id=(c_me, to), device_id_type=MESH,
         )
 
-    for ch in range(len(COLUMNS)):
+    def relay(which, j, back_by):
+        step = 1 if back_by == 0 else -1
+        if which == 0:
+            ref = place_of(ring(y, -step, other), ring(z, -j, side), 0, 0)
+            to = ring(y, step, other) * side + z
+        else:
+            ref = place_of(ring(y, -j, other), ring(z, -step, side), 1, 0)
+            to = y * side + ring(z, step, side)
+        ref = ref.at[pl.ds(back_by * quarter, quarter)]
+        return pltpu.make_async_remote_copy(
+            ref, ref, sem_rel.at[which, j, back_by, 0], sem_rel.at[which, j, back_by, 1],
+            device_id=(c_me, to), device_id_type=MESH,
+        )
+
+    for ch in range(2):
         for k in (1, 3, 2):
             near(ch, 0, k).start()
             near(ch, 1, k).start()
-        for k in (1, 3, 2):
+        for k in (1, 3) if ch == 0 else (1, 3, 2):
             forward(ch, 0, 0, k).start()
             forward(ch, 1, 0, k).start()
-    gather_own = pltpu.make_async_copy(
-        joined, jr.at[pl.ds(pl.multiple_of(d_me * tok, tok), tok)], sem_own.at[0]
-    )
+    gather_own = [
+        pltpu.make_async_copy(ja, ga.at[pl.ds(pl.multiple_of(d_me * tok, tok), tok)], sem_own.at[0]),
+        pltpu.make_async_copy(jb, gb.at[d_me], sem_own.at[1]),
+    ]
     hidden_own.wait()
-    gather_own.start()
+    for c in gather_own:
+        c.start()
     each(2, lambda i: late_queries(i + 2))
     send_out(last, 1)
-    for ch in range(len(COLUMNS)):
-        for j in (1, 3, 2):
-            for which in range(2):
-                near(ch, which, j).wait_recv()
-                for k in (1, 3, 2):
-                    forward(ch, which, j, k).start()
+    for j in (1, 3, 2):
+        for which in range(2):
+            near(0, which, j).wait_recv()
+            for k in (1, 3):
+                forward(0, which, j, k).start()
+    for j in (0, 1, 3, 2):
+        for which in range(2):
+            for k in (1, 3):
+                forward(0, which, j, k).wait_recv()
+                relay(which, j, k // 2).start()
+    for j in (1, 3, 2):
+        for which in range(2):
+            near(1, which, j).wait_recv()
+            for k in (1, 3, 2):
+                forward(1, which, j, k).start()
     each(ndp - 1, lambda i: hidden_copy(i).wait())
-    gather_own.wait()
+    for c in gather_own:
+        c.wait()
+    for j in (0, 1, 3, 2):
+        for which in range(2):
+            for back_by in range(2):
+                relay(which, j, back_by).wait_recv()
 
     def part_copy(ch, i):
         to = cp_dev(i + 1)
+        src, dst = ((pa, ra), (pb, rb))[ch]
         return pltpu.make_async_remote_copy(
-            part.at[pl.ds(pl.multiple_of(to * PIECE, PIECE), PIECE), COLUMNS[ch]],
-            parts.at[i, :, COLUMNS[ch]],
-            sem_ps.at[ch, i], sem_pr.at[ch, i], device_id=(to, d_me), device_id_type=MESH,
+            src.at[to], dst.at[i], sem_ps.at[ch, i], sem_pr.at[ch, i],
+            device_id=(to, d_me), device_id_type=MESH,
         )
 
-    for ch in range(len(COLUMNS)):
-        for j in range(4):
-            for which in range(2):
-                for k in (1, 2, 3):
-                    forward(ch, which, j, k).wait_recv()
-
-        def product(c):
-            piece = pl.ds(pl.multiple_of(c * 256, 256), 256)
-            part[piece, COLUMNS[ch]] = dot(hr[piece, :], jr[:, COLUMNS[ch]], 1, 0).astype(BF)
-
-        each(part.shape[0] // 256, product)
-        each(ncp - 1, lambda i: part_copy(ch, i).start())
-    for ch in range(len(COLUMNS)):
-        cols = COLUMNS[ch]
-        mine = part[pl.ds(pl.multiple_of(c_me * PIECE, PIECE), PIECE), cols].astype(F32)
-        for i in range(ncp - 1):
-            part_copy(ch, i).wait_recv()
-            mine = mine + parts[i, :, cols].astype(F32)
-        width_now = min(cols.stop, lat + ROPE) - cols.start
-        dw[:, cols.start : cols.start + width_now] = mine[:rows_dev, :width_now]
-
+    block = 4 * PIECE
+
+    def product(c):
+        d = dot(hr[pl.ds(pl.multiple_of(c * block, block), block), :], ga[...], 1, 0).astype(BF)
+        for i in range(4):
+            pa[c * 4 + i] = d[i * PIECE : (i + 1) * PIECE]
+
+    each(ncp // 4, product)
+    each(ncp - 1, lambda i: part_copy(0, i).start())
+    for j in range(4):
+        for which in range(2):
+            for k in (1, 2, 3):
+                forward(1, which, j, k).wait_recv()
+
+    def unfold(i):
+        for w in range(2):
+            at = i * tok + w * half
+            gc[pl.ds(pl.multiple_of(at, half), half), :128] = gb[i, w, :half, :]
+            folded = gb[i, w, half:, :].astype(F32)
+            gc[pl.ds(pl.multiple_of(at, quarter), quarter), 128:] = folded.astype(BF)
+            gc[pl.ds(pl.multiple_of(at + quarter, quarter), quarter), 128:] = pltpu.roll(folded, ROPE, 1).astype(BF)
+
+    each(ndp, unfold)
+
+    def product_rest(c):
+        d = dot(hr[pl.ds(pl.multiple_of(c * block, block), block), :], gc[...], 1, 0)
+        for i in range(4):
+            piece = d[i * PIECE : (i + 1) * PIECE]
+            pb[c * 4 + i, :PIECE, :] = piece[:, :128].astype(BF)
+            folded = jnp.where(low[: PIECE // 2], piece[: PIECE // 2, 128:], pltpu.roll(piece[PIECE // 2 :, 128:], ROPE, 1))
+            pb[c * 4 + i, PIECE:, :] = folded.astype(BF)
+
+    each(ncp // 4, product_rest)
+    each(ncp - 1, lambda i: part_copy(1, i).start())
     for c in halo + back_copies:
         c.wait_send()
-    for ch in range(len(COLUMNS)):
-        for which in range(2):
+    for which in range(2):
+        for ch in range(2):
             for k in (1, 2, 3):
                 near(ch, which, k).wait_send()
             for j in range(4):
-                for k in (1, 2, 3):
+                for k in (1, 3) if ch == 0 else (1, 2, 3):
                     forward(ch, which, j, k).wait_send()
+        for j in range(4):
+            for back_by in range(2):
+                relay(which, j, back_by).wait_send()
+    first = pa[c_me].astype(F32)
+    for i in range(ncp - 1):
+        part_copy(0, i).wait_recv()
+        first = first + ra[i].astype(F32)
+    dw[:, :FIRST] = first[:rows_dev]
+    rest = pb[c_me].astype(F32)
+    for i in range(ncp - 1):
+        part_copy(1, i).wait_recv()
+        rest = rest + rb[i].astype(F32)
+    dw[:, FIRST:lat] = rest[:rows_dev]
+    dw[: PIECE // 2, lat:] = rest[PIECE:, :ROPE]
+    dw[PIECE // 2 :, lat:] = pltpu.roll(rest[PIECE:], ROPE, 1)[: rows_dev - PIECE // 2, :ROPE]
+
+    for ch in range(2):
         each(ncp - 1, lambda i: part_copy(ch, i).wait_send())
 
     def finish(n):
@@ -524,9 +610,9 @@
             pltpu.VMEM((tok, model), BF),
             pltpu.VMEM(w_uk.shape, BF),
             pltpu.VMEM(w_uv.shape, BF),
-            pltpu.VMEM((layers, rows, head), F32),
-            pltpu.VMEM((layers, rows, head), F32),
-            pltpu.VMEM((ncp, rows // ncp // 2, head), F32),
+            pltpu.VMEM((layers, tok * PITCH, head), F32),
+            pltpu.VMEM((layers, tok * PITCH, head), F32),
+            pltpu.VMEM((ncp, tok // ncp * OUT_PITCH, head), F32),
             pltpu.VMEM((ncp, tok // ncp, wide // 2), BF),
             pltpu.VMEM((2, 2, HG * SUB, ext), BF),
             pltpu.VMEM((2, 2, HG * SUB, lat), BF),
@@ -542,10 +628,15 @@
             pltpu.VMEM((MARGIN, ext), BF),
             pltpu.VMEM((tok, ext), BF),
             pltpu.VMEM((MARGIN - tok, ext), BF),
-            pltpu.VMEM((tok, ext), BF),
-            pltpu.VMEM((ndp * tok, ext), BF),
-            pltpu.VMEM((ncp * PIECE, ext), BF),
-            pltpu.VMEM((ncp - 1, PIECE, ext), BF),
+            pltpu.VMEM((tok, FIRST), BF),
+            pltpu.VMEM((2, tok // 2 + tok // 4, 128), BF),
+            pltpu.VMEM((ndp * tok, FIRST), BF),
+            pltpu.VMEM((ndp, 2, tok // 2 + tok // 4, 128), BF),
+            pltpu.VMEM((ndp * tok, 256), BF),
+            pltpu.VMEM((ncp, PIECE, FIRST), BF),
+            pltpu.VMEM((ncp, PIECE + PIECE // 2, 128), BF),
+            pltpu.VMEM((ncp - 1, PIECE, FIRST), BF),
+            pltpu.VMEM((ncp - 1, PIECE + PIECE // 2, 128), BF),
             dma((layers, 3)),
             dma((layers, heads // HG, 2)),
             dma((3,)),
@@ -556,12 +647,13 @@
             dma((layers, 2, ncp - 1, 2)),
             dma((layers, 2, 2)),
             dma((4,)),
-            dma((len(COLUMNS), 2, 2, 3)),
-            dma((len(COLUMNS), 2, 4, 3)),
-            dma((len(COLUMNS), 2, 4, 3)),
-            dma((len(COLUMNS), ncp - 1)),
-            dma((len(COLUMNS), ncp - 1)),
-            dma((1,)),
+            dma((2, 2, 2, 3)),
+            dma((2, 2, 4, 3)),
+            dma((2, 2, 4, 3)),
+            dma((2, 4, 2, 2)),
+            dma((2, ncp - 1)),
+            dma((2, ncp - 1)),
+            dma((2,)),
         ],
         compiler_params=pltpu.CompilerParams(
             collective_id=0, has_side_effects=True, vmem_limit_bytes=60 * 1024 * 1024

time: 88.3 us -> 81 us (0.917); the launches traced: 88.2 us -> 79.9 us
  Pallas kernels: 87.5 us -> 79.3 us
    pallas_call x1, Pallas kernels: 84.1 us -> 75.9 us  [on_device(): pl.pallas_call(functools.partial(kernel, ncp, ndp, side), out_shape=(jax....]
where the time goes in v4:
time: 81 us; the launch traced here: 79.9 us
  Pallas kernels  79.3 us (98%)
    pallas_call x1, Pallas kernels, on_device(): pl.pallas_call(functools.partial(kernel, ncp, ndp, side), out_shape=(jax....  75.9 us
    pallas_call x1, Pallas kernels, on_device(): pl.pallas_call(pass_on, out_shape=tuple((jax.ShapeDtypeStruct(r.shape, r....  3.41 us

profile of v4, /device:TPU:1, one launch (start us, length us, event | category | flops | bytes accessed | tf_op | source)
XLA Modules:
  0.0 79.9 jit_solution(8886935897845380890)
XLA Ops:
  0.6 75.9 %attention_backward.1 = (bf16[2,128,32,128]{3,2,1,0:T(8,128)(2,1)}, bf16[2,128,2048]{2,1,0:T(8,128)(2,1)}, bf16[128,512]{1,0:T(8,128)(2,1)}, bf16[64,128]{1,0:T(8,128)(2,1)}, f32[56,576]{1,0:T(8,128)}) custom-call(s32[1,32]{1,0:T(1,128)} %lens.1, s32[1,8,8]{2,1,0:T(8,128)} %plan.1, bf16[2,4096,128]{2,1,0:T(8,128)(2,1)} %bitcast.14, ...), custom_call_target="tpu_custom_call" | custom-call | tf_op jit(solution)/shard_map/attention_backward/pallas_call | solution.py:593
  76.5 3.4 %pass_on.1 = (bf16[2,128,32,128]{3,2,1,0:T(8,128)(2,1)}, bf16[2,128,2048]{2,1,0:T(8,128)(2,1)}, bf16[128,512]{1,0:T(8,128)(2,1)}, bf16[64,128]{1,0:T(8,128)(2,1)}, f32[56,576]{1,0:T(8,128)}) custom-call(bf16[2,128,32,128]{3,2,1,0:T(8,128)(2,1)} %get-tuple-element.15.refs_0_, bf16[2,128,2048]{2,1,0:T(8,128)(2,1)} %get-tuple-element.16.refs_1_, ...), custom_call_target="tpu_custom_call" | custom-call | tf_op jit(solution)/shard_map/pass_on/pallas_call | solution.py:674

commit v5 on v4

--- a/solution.py
+++ b/solution.py
@@ -83,7 +83,7 @@
         pltpu.make_async_copy(kr_h, kr, sem_k.at[1]),
         pltpu.make_async_copy(hid_h, hid, sem_k.at[2]),
     ]
-    for c in k_copies[:2] + q_copies(0) + w_copies(0, 0):
+    for c in k_copies + q_copies(0) + w_copies(0, 0):
         c.start()
 
     barrier = pltpu.get_barrier_semaphore()
@@ -115,6 +115,35 @@
     ]
     for c in halo:
         c.start()
+
+    k_copies[2].wait()
+    width = hid.shape[1] // ncp
+    rows_dev = width // ndp
+
+    def turn(c):
+        for j in range(width // 128):
+            lanes = pl.ds(pl.multiple_of(c * width + j * 128, 128), 128)
+            slab[j * 128 : j * 128 + 128, :] = hid[:, lanes].astype(F32).T
+        pad = jnp.zeros((PIECE - rows_dev, tok), F32)
+        for j in range(ndp):
+            piece = jnp.concatenate([slab[j * rows_dev : (j + 1) * rows_dev, :], pad], axis=0)
+            ht[j, pl.ds(pl.multiple_of(c * PIECE, PIECE), PIECE), :] = piece.astype(BF)
+
+    each(ncp, turn)
+
+    def my_lanes():
+        return pl.ds(pl.multiple_of(d_me * tok, tok), tok)
+
+    def hidden_copy(i):
+        to = dp_dev(i + 1)
+        return pltpu.make_async_remote_copy(
+            ht.at[to], hr.at[:, my_lanes()], sem_hs.at[i], sem_hr.at[i],
+            device_id=(c_me, to), device_id_type=MESH,
+        )
+
+    each(ndp - 1, lambda i: hidden_copy(i).start())
+    hidden_own = pltpu.make_async_copy(ht.at[d_me], hr.at[:, my_lanes()], sem_own.at[0])
+    hidden_own.start()
 
     acc[...] = jnp.zeros_like(acc)
     for s in range(2):
@@ -272,8 +301,9 @@
                 x, p = softmax(s, score, dprob, j)
                 ds.append(x)
                 low_p.append(p)
-                if more:
-                    absorb(follow, 1 - slot, s * (HG // 2) + j)
+                if more and s == 0:
+                    absorb(follow, 1 - slot, 2 * j)
+                    absorb(follow, 1 - slot, 2 * j + 1)
             ds = jnp.concatenate(ds, axis=0)
             low_p = jnp.concatenate(low_p, axis=0)
             if defer:
@@ -300,7 +330,7 @@
     ]
 
     widen(0)
-    for c in k_copies[2:] + w_copies(0, 1):
+    for c in w_copies(0, 1):
         c.start()
     for c in w_copies(0, 0):
         c.wait()
@@ -308,36 +338,6 @@
         c.start()
     for i in range(HG):
         absorb(jnp.int32(0), 0, i)
-
-    k_copies[2].wait()
-    width = hid.shape[1] // ncp
-    rows_dev = width // ndp
-
-    def turn(c):
-        for j in range(width // 128):
-            lanes = pl.ds(pl.multiple_of(c * width + j * 128, 128), 128)
-            slab[j * 128 : j * 128 + 128, :] = hid[:, lanes].astype(F32).T
-        pad = jnp.zeros((PIECE - rows_dev, tok), F32)
-        for j in range(ndp):
-            piece = jnp.concatenate([slab[j * rows_dev : (j + 1) * rows_dev, :], pad], axis=0)
-            ht[j, pl.ds(pl.multiple_of(c * PIECE, PIECE), PIECE), :] = piece.astype(BF)
-
-    each(ncp, turn)
-
-    def my_lanes():
-        return pl.ds(pl.multiple_of(d_me * tok, tok), tok)
-
-    def hidden_copy(i):
-        to = dp_dev(i + 1)
-        return pltpu.make_async_remote_copy(
-            ht.at[to], hr.at[:, my_lanes()], sem_hs.at[i], sem_hr.at[i],
-            device_id=(c_me, to), device_id_type=MESH,
-        )
-
-    each(ndp - 1, lambda i: hidden_copy(i).start())
-    hidden_own = pltpu.make_async_copy(ht.at[d_me], hr.at[:, my_lanes()], sem_own.at[0])
-    hidden_own.start()
-
     for c in halo:
         c.wait_recv()
 

time: 81 us -> 78.9 us (0.974); the launches traced: 79.9 us -> 78.7 us
  Pallas kernels: 79.3 us -> 78.1 us
    pallas_call x1, Pallas kernels: 75.9 us -> 74.7 us  [on_device(): pl.pallas_call(functools.partial(kernel, ncp, ndp, side), out_shape=(jax....]
where the time goes in v5:
time: 78.9 us; the launch traced here: 78.7 us
  Pallas kernels  78.1 us (99%)
    pallas_call x1, Pallas kernels, on_device(): pl.pallas_call(functools.partial(kernel, ncp, ndp, side), out_shape=(jax....  74.7 us
    pallas_call x1, Pallas kernels, on_device(): pl.pallas_call(pass_on, out_shape=tuple((jax.ShapeDtypeStruct(r.shape, r....  3.41 us

profile of v5, /device:TPU:1, one launch (start us, length us, event | category | flops | bytes accessed | tf_op | source)
XLA Modules:
  0.0 78.7 jit_solution(8281630532096686983)
XLA Ops:
  0.6 74.7 %attention_backward.1 = (bf16[2,128,32,128]{3,2,1,0:T(8,128)(2,1)}, bf16[2,128,2048]{2,1,0:T(8,128)(2,1)}, bf16[128,512]{1,0:T(8,128)(2,1)}, bf16[64,128]{1,0:T(8,128)(2,1)}, f32[56,576]{1,0:T(8,128)}) custom-call(s32[1,32]{1,0:T(1,128)} %lens.1, s32[1,8,8]{2,1,0:T(8,128)} %plan.1, bf16[2,4096,128]{2,1,0:T(8,128)(2,1)} %bitcast.14, ...), custom_call_target="tpu_custom_call" | custom-call | tf_op jit(solution)/shard_map/attention_backward/pallas_call | solution.py:593
  75.3 3.4 %pass_on.1 = (bf16[2,128,32,128]{3,2,1,0:T(8,128)(2,1)}, bf16[2,128,2048]{2,1,0:T(8,128)(2,1)}, bf16[128,512]{1,0:T(8,128)(2,1)}, bf16[64,128]{1,0:T(8,128)(2,1)}, f32[56,576]{1,0:T(8,128)}) custom-call(bf16[2,128,32,128]{3,2,1,0:T(8,128)(2,1)} %get-tuple-element.15.refs_0_, bf16[2,128,2048]{2,1,0:T(8,128)(2,1)} %get-tuple-element.16.refs_1_, ...), custom_call_target="tpu_custom_call" | custom-call | tf_op jit(solution)/shard_map/pass_on/pallas_call | solution.py:674

commit v6 on v5

--- a/solution.py
+++ b/solution.py
@@ -610,9 +610,9 @@
             pltpu.VMEM((tok, model), BF),
             pltpu.VMEM(w_uk.shape, BF),
             pltpu.VMEM(w_uv.shape, BF),
-            pltpu.VMEM((layers, tok * PITCH, head), F32),
-            pltpu.VMEM((layers, tok * PITCH, head), F32),
-            pltpu.VMEM((ncp, tok // ncp * OUT_PITCH, head), F32),
+            pltpu.VMEM((layers, tok * PITCH + 40, head), F32),
+            pltpu.VMEM((layers, tok * PITCH + 40, head), F32),
+            pltpu.VMEM((ncp, tok // ncp * OUT_PITCH + 24, head), F32),
             pltpu.VMEM((ncp, tok // ncp, wide // 2), BF),
             pltpu.VMEM((2, 2, HG * SUB, ext), BF),
             pltpu.VMEM((2, 2, HG * SUB, lat), BF),

time: 78.9 us -> 78.9 us (level)
  no operation moved by 1% of the time
where the time goes in v6:
time: 78.9 us; the launch traced here: 78.7 us
  Pallas kernels  78.1 us (99%)
    pallas_call x1, Pallas kernels, on_device(): pl.pallas_call(functools.partial(kernel, ncp, ndp, side), out_shape=(jax....  74.7 us
    pallas_call x1, Pallas kernels, on_device(): pl.pallas_call(pass_on, out_shape=tuple((jax.ShapeDtypeStruct(r.shape, r....  3.41 us

profile of v6, /device:TPU:1, one launch (start us, length us, event | category | flops | bytes accessed | tf_op | source)
XLA Modules:
  0.0 78.7 jit_solution(2043105811521727073)
XLA Ops:
  0.6 74.7 %attention_backward.1 = (bf16[2,128,32,128]{3,2,1,0:T(8,128)(2,1)}, bf16[2,128,2048]{2,1,0:T(8,128)(2,1)}, bf16[128,512]{1,0:T(8,128)(2,1)}, bf16[64,128]{1,0:T(8,128)(2,1)}, f32[56,576]{1,0:T(8,128)}) custom-call(s32[1,32]{1,0:T(1,128)} %lens.1, s32[1,8,8]{2,1,0:T(8,128)} %plan.1, bf16[2,4096,128]{2,1,0:T(8,128)(2,1)} %bitcast.14, ...), custom_call_target="tpu_custom_call" | custom-call | tf_op jit(solution)/shard_map/attention_backward/pallas_call | solution.py:593
  75.3 3.4 %pass_on.1 = (bf16[2,128,32,128]{3,2,1,0:T(8,128)(2,1)}, bf16[2,128,2048]{2,1,0:T(8,128)(2,1)}, bf16[128,512]{1,0:T(8,128)(2,1)}, bf16[64,128]{1,0:T(8,128)(2,1)}, f32[56,576]{1,0:T(8,128)}) custom-call(bf16[2,128,32,128]{3,2,1,0:T(8,128)(2,1)} %get-tuple-element.15.refs_0_, bf16[2,128,2048]{2,1,0:T(8,128)(2,1)} %get-tuple-element.16.refs_1_, ...), custom_call_target="tpu_custom_call" | custom-call | tf_op jit(solution)/shard_map/pass_on/pallas_call | solution.py:674
